TPU v7x, 256 devices: a whole 4x4x8 slice. The times are simulated.
256 devices in a mesh: view: 64 (over z, x, core), seq: 4 (over y).
Axes of the slice: x: 4, y: 4, z: 8, core: 2. Of those that a mesh axis runs over, the one named last changes fastest.
Arguments:
- queries: bfloat16 [64, 768, 1024], P('view', 'seq'), may hold values from -6 to 6
- keys: bfloat16 [64, 768, 1024], P('view', 'seq'), may hold values from -6 to 6
- values: bfloat16 [64, 768, 1024], P('view', 'seq'), may hold values from -6 to 6
- out_grad: bfloat16 [64, 768, 1024], P('view', 'seq'), may hold values from -6 to 6
- nbr_views: int32 [64, 3], P('view'), may hold values from 0 to 63, as said below
- nbr_counts: int32 [64], P('view'), may hold values from 1 to 3, as said below
Outputs:
- attended: bfloat16 [64, 768, 1024], P('view', 'seq')
- grad_q: bfloat16 [64, 768, 1024], P('view', 'seq')
- grad_k: bfloat16 [64, 768, 1024], P('view', 'seq')
- grad_v: bfloat16 [64, 768, 1024], P('view', 'seq')
Inputs may be any that keep to these rules, and one draw needn't show every extreme that they name: `nbr_views`: views v with equal v // 16 form a scene. The 3 entries of view v's list are distinct views of v's scene, other than v, at most 4 views away from v. Only the first nbr_counts[v] entries of view v's list are its neighbours.
All inputs are finite; a program needn't handle non-finite values.
Results may differ from a plain program's by a relative error of at most 0.034.
Values may be sent and summed in bfloat16 or wider, within the bound.
No kernel may reach another device: no remote copies, remote signals or barrier semaphores. Data moves between devices by JAX's collectives and lax.ppermute only.
A program may use at most 128 MiB of HBM per device.

v0:
```python
import functools

import jax
import jax.numpy as jnp
from jax import lax
from jax.experimental import pallas as pl
from jax.experimental.pallas import tpu as pltpu
from jax.sharding import Mesh, PartitionSpec as P

HEAD_DIM = 64
PAIR = 2 * HEAD_DIM
HEADS = 16
TOK = 768
PIECE = 192
ROW = 4
EDGE = 2
MAXNB = 3
SCALE = HEAD_DIM ** (-0.5)
BF = jnp.bfloat16
F32 = jnp.float32
VMEM_LIMIT = 60 * 1024 * 1024


def pack_kernel(a_ref, b_ref, out_ref):
    for h in range(out_ref.shape[0]):
        cols = slice(h * HEAD_DIM, (h + 1) * HEAD_DIM)
        out_ref[h] = jnp.concatenate([a_ref[:, cols], b_ref[:, cols]], axis=1)


def pack(a, b):
    steps = 4
    return pl.pallas_call(
        pack_kernel,
        grid=(steps,),
        in_specs=[pl.BlockSpec((PIECE, HEADS * HEAD_DIM // steps), lambda i: (0, i))] * 2,
        out_specs=pl.BlockSpec((HEADS // steps, PIECE, PAIR), lambda i: (i, 0, 0)),
        out_shape=jax.ShapeDtypeStruct((HEADS, PIECE, PAIR), BF),
    )(a, b)


def unpack_kernel(in_ref, a_ref, b_ref):
    for h in range(in_ref.shape[0]):
        cols = slice(h * HEAD_DIM, (h + 1) * HEAD_DIM)
        a_ref[:, cols] = in_ref[h, :, :HEAD_DIM]
        b_ref[:, cols] = in_ref[h, :, HEAD_DIM:]


def unpack(packed):
    steps = 4
    whole = jax.ShapeDtypeStruct((PIECE, HEADS * HEAD_DIM), BF)
    return pl.pallas_call(
        unpack_kernel,
        grid=(steps,),
        in_specs=[pl.BlockSpec((HEADS // steps, PIECE, PAIR), lambda i: (i, 0, 0))],
        out_specs=[pl.BlockSpec((PIECE, HEADS * HEAD_DIM // steps), lambda i: (0, i))] * 2,
        out_shape=[whole, whole],
    )(packed)


def dot(a, b):
    return jnp.dot(a, b, preferred_element_type=F32)


def attention_kernel(
    index_ref, count_ref, qg_ref, own_ref, edge_ref, mate_ref, mate_edge_ref,
    od_ref, dkv_ref,
    kv, kv_t, ones_v, total, expo, low, outs, tops, sem,
):
    copies = [
        pltpu.make_async_copy(own_ref, kv.at[0:ROW], sem.at[0]),
        pltpu.make_async_copy(edge_ref, kv.at[ROW : ROW + EDGE], sem.at[1]),
        pltpu.make_async_copy(mate_ref, kv.at[ROW + EDGE : 2 * ROW + EDGE], sem.at[2]),
        pltpu.make_async_copy(mate_edge_ref, kv.at[2 * ROW + EDGE : 2 * (ROW + EDGE)], sem.at[3]),
    ]
    for copy in copies:
        copy.start()
    for copy in copies:
        copy.wait()

    lane = lax.broadcasted_iota(jnp.int32, (TOK, PAIR), 1)
    sub = lax.broadcasted_iota(jnp.int32, (PAIR, TOK), 0)

    def prepare(i, carry):
        block = kv[i]
        kv_t[i, :PAIR, :] = block.T
        kv_t[i, PAIR:, :] = jnp.ones((16, TOK), BF)
        ones_v[i] = jnp.where(lane < HEAD_DIM, jnp.ones_like(block), block)
        total[i] = jnp.zeros((TOK, PAIR), F32)
        return carry

    lax.fori_loop(0, 2 * (ROW + EDGE), prepare, 0)

    def one_view(j, carry):
        qg = qg_ref[j]
        qg_t = qg.T
        q_t = jnp.where(sub < HEAD_DIM, qg_t * SCALE, jnp.zeros_like(qg_t)).astype(BF)
        used = 1 + count_ref[j]

        def forward(b, carry):
            top, acc = carry
            i = index_ref[j, b]
            scores = dot(kv[i], q_t)
            top_b = jnp.max(scores, axis=0, keepdims=True)
            e = jnp.exp(scores - top_b).astype(BF)
            expo[b] = e
            part = dot(kv_t[i, HEAD_DIM:, :], e)
            tops[b, :, :] = top_b
            new = jnp.maximum(top, top_b)
            acc = acc * jnp.exp(top - new) + part * jnp.exp(top_b - new)
            return new, acc

        top, acc = lax.fori_loop(
            0, used, forward,
            (jnp.full((1, TOK), -jnp.inf, F32), jnp.zeros((HEAD_DIM + 16, TOK), F32)),
        )
        inverse = 1.0 / acc[HEAD_DIM : HEAD_DIM + 1]
        att = acc[:HEAD_DIM] * inverse
        delta = jnp.sum(qg_t[HEAD_DIM:].astype(F32) * att, axis=0, keepdims=True)
        d_hi = delta.astype(BF)
        d_mid = (delta - d_hi.astype(F32)).astype(BF)
        d_lo = (delta - d_hi.astype(F32) - d_mid.astype(F32)).astype(BF)
        g_t = jnp.where(
            sub == 0, -d_hi,
            jnp.where(sub == 1, -d_mid,
                      jnp.where(sub == 2, -d_lo,
                                jnp.where(sub < HEAD_DIM, jnp.zeros_like(qg_t), qg_t))),
        )
        q_side = jnp.where(lane < HEAD_DIM, qg * SCALE, jnp.zeros_like(qg)).astype(BF)
        g_side = jnp.where(lane < HEAD_DIM, jnp.zeros_like(qg), qg)

        def backward(b, dq):
            i = index_ref[j, b]
            share = jnp.exp(tops[b] - top) * inverse
            dprobs = dot(ones_v[i], g_t)
            p = expo[b].astype(F32) * share
            ds = (p * dprobs).astype(BF)
            dq = dq + dot(kv_t[i, :HEAD_DIM, :], ds)
            total[i] += dot(ds, q_side) + dot(p.astype(BF), g_side)
            return dq

        dq = lax.fori_loop(0, used, backward, jnp.zeros((HEAD_DIM, TOK), F32))
        od = jnp.concatenate([att.astype(BF), (dq * SCALE).astype(BF)], axis=0)
        od_ref[j] = od.T
        return carry

    lax.fori_loop(0, ROW, one_view, 0)

    def emit(i, carry):
        dkv_ref[i] = total[i].astype(BF)
        return carry

    lax.fori_loop(0, 2 * (ROW + EDGE), emit, 0)


def attention(index, count, qg, own, edge, mate, mate_edge):
    window = 2 * (ROW + EDGE)
    hbm = pl.BlockSpec(memory_space=pl.ANY)
    smem = pl.BlockSpec(memory_space=pltpu.SMEM)
    vmem = pl.BlockSpec(memory_space=pltpu.VMEM)
    return pl.pallas_call(
        attention_kernel,
        in_specs=[smem, smem, vmem, hbm, hbm, hbm, hbm],
        out_specs=[vmem, vmem],
        out_shape=[
            jax.ShapeDtypeStruct((ROW, TOK, PAIR), BF),
            jax.ShapeDtypeStruct((window, TOK, PAIR), BF),
        ],
        scratch_shapes=[
            pltpu.VMEM((window, TOK, PAIR), BF),
            pltpu.VMEM((window, PAIR + 16, TOK), BF),
            pltpu.VMEM((window, TOK, PAIR), BF),
            pltpu.VMEM((window, TOK, PAIR), F32),
            pltpu.VMEM((1 + MAXNB, TOK, TOK), BF),
            pltpu.VMEM((TOK, 2 * TOK), BF),
            pltpu.VMEM((HEAD_DIM, TOK), F32),
            pltpu.VMEM((1 + MAXNB, 1, TOK), F32),
            pltpu.SemaphoreType.DMA((4,)),
        ],
        compiler_params=pltpu.CompilerParams(vmem_limit_bytes=VMEM_LIMIT),
    )(index, count, qg, own, edge, mate, mate_edge)


def block_index(nbr_views, nbr_counts):
    z, x, c = lax.axis_index("z"), lax.axis_index("x"), lax.axis_index("c")
    at = nbr_views[0] % (4 * ROW)
    same_row = (at // (2 * ROW)) == (z % 2)
    column = (at // 2) % ROW
    place = jnp.where(same_row, column, ROW + column % 2)
    place = jnp.where(at % 2 == c, place, place + ROW + EDGE)
    mine = jnp.concatenate([x[None].astype(jnp.int32), place, nbr_counts])
    everyone = lax.all_gather(mine, "x")
    return everyone[:, : 1 + MAXNB], everyone[:, 1 + MAXNB]


def local(queries, keys, values, out_grad, nbr_views, nbr_counts):
    index, count = block_index(nbr_views, nbr_counts)
    kv = pack(keys[0], values[0])
    qg = pack(queries[0], out_grad[0])
    own = lax.all_to_all(kv, ("x", "y"), 0, 0, tiled=True).reshape(ROW, TOK, PAIR)
    qg = lax.all_to_all(qg, ("x", "y"), 0, 0, tiled=True).reshape(ROW, TOK, PAIR)
    cores = [(0, 1), (1, 0)]
    rows = [(i, i ^ 1) for i in range(lax.axis_size("z"))]
    upper = lax.axis_index("z") % 2 == 1
    start = jnp.where(upper, 0, ROW - EDGE)
    edge = lax.ppermute(lax.dynamic_slice_in_dim(own, start, EDGE, 0), "z", rows)
    mate = lax.ppermute(own, "c", cores)
    mate_edge = lax.ppermute(edge, "c", cores)
    od, dkv = attention(index, count, qg, own, edge, mate, mate_edge)
    od = lax.all_to_all(od.reshape(HEADS, PIECE, PAIR), ("x", "y"), 0, 0, tiled=True)
    attended, grad_q = unpack(od)
    got = lax.ppermute(dkv[ROW + EDGE :], "c", cores)
    edge_sum = (dkv[ROW : ROW + EDGE].astype(F32) + got[ROW:].astype(F32)).astype(BF)
    edge_got = lax.ppermute(edge_sum, "z", rows)
    own_sum = dkv[:ROW].astype(F32) + got[:ROW].astype(F32)
    zero = jnp.zeros_like(edge_got)
    edge_full = jnp.concatenate(
        [jnp.where(upper, edge_got, zero), jnp.where(upper, zero, edge_got)], axis=0
    )
    dkv_sum = (own_sum + edge_full.astype(F32)).astype(BF)
    back = lax.all_to_all(dkv_sum.reshape(HEADS, PIECE, PAIR), ("x", "y"), 0, 0, tiled=True)
    grad_k, grad_v = unpack(back)
    return attended[None], grad_q[None], grad_k[None], grad_v[None]


def solution(mesh):
    fine = Mesh(mesh.devices.reshape(8, 4, 2, 4), ("z", "x", "c", "y"))
    views = ("z", "x", "c")
    tokens = P(views, "y", None)
    return jax.shard_map(
        local,
        mesh=fine,
        in_specs=(tokens, tokens, tokens, tokens, P(views, None), P(views)),
        out_specs=(tokens, tokens, tokens, tokens),
        check_vma=False,
    )
```

profile of v0, /device:TPU:64, one launch (start us, length us, event | category | flops | bytes accessed | tf_op | source)
XLA Modules:
  0.0 142.6 jit_solution(14047901577188440402)
XLA Ops:
  0.6 3.5 %shard_map.94 = bf16[16,192,128]{2,1,0:T(8,128)(2,1)} custom-call(bf16[192,1024]{1,0:T(8,128)(2,1)} %bitcast.24, bf16[192,1024]{1,0:T(8,128)(2,1)} %bitcast.25), custom_call_target="tpu_custom_call" | custom-call | tf_op jit(solution)/shard_map/pallas_call | solution.py:32
  4.1 7.0 %all-to-all-start.1 = ((bf16[16,192,128]{2,1,0:T(8,128)(2,1)}), bf16[16,192,128]{2,1,0:T(8,128)(2,1)S(1)}, u32[]{:S(2)}, u32[]{:S(2)}) async-start(bf16[16,192,128]{2,1,0:T(8,128)(2,1)} %shard_map.94), calls=%async_computation.1 | async-start | bytes 1572864 | tf_op jit(solution)/shard_map/all_to_all | solution.py:199
  11.2 14.3 %all-to-all-done.1 = bf16[16,192,128]{2,1,0:T(8,128)(2,1)S(1)} async-done(((bf16[16,192,128]{2,1,0:T(8,128)(2,1)}), bf16[16,192,128]{2,1,0:T(8,128)(2,1)S(1)}, u32[]{:S(2)}, u32[]{:S(2)}) %all-to-all-start.1) | async-done | bytes 786464 | tf_op jit(solution)/shard_map/all_to_all | solution.py:199
  25.6 2.0 %collective-permute-start = (bf16[2,768,128]{2,1,0:T(8,128)(2,1)S(1)}, bf16[2,768,128]{2,1,0:T(8,128)(2,1)S(1)}, u32[]{:S(2)}, u32[]{:S(2)}) collective-permute-start(bf16[2,768,128]{2,1,0:T(8,128)(2,1)S(1)} %constant_dynamic-slice_fusion), channel_id=1, source_target_pairs={{0,32},{32,0},{64,96},{96,64},{128,160},{160,128},{192,224},{224,1... | collective-permute-start | bytes 1179656 | tf_op jit(solution)/shard_map/ppermute | solution.py:205
  27.6 0.0 collective-permute-start.1
  27.6 3.5 %shard_map.93 = bf16[16,192,128]{2,1,0:T(8,128)(2,1)} custom-call(bf16[192,1024]{1,0:T(8,128)(2,1)} %bitcast.26, bf16[192,1024]{1,0:T(8,128)(2,1)} %bitcast.27), custom_call_target="tpu_custom_call" | custom-call | tf_op jit(solution)/shard_map/pallas_call | solution.py:32
  31.1 0.0 copy-done
  31.1 3.6 %all-to-all-start = ((bf16[16,192,128]{2,1,0:T(8,128)(2,1)}), bf16[16,192,128]{2,1,0:T(8,128)(2,1)S(1)}, u32[]{:S(2)}, u32[]{:S(2)}) async-start(bf16[16,192,128]{2,1,0:T(8,128)(2,1)} %shard_map.93), calls=%async_computation | async-start | bytes 1572864 | tf_op jit(solution)/shard_map/all_to_all | solution.py:200
  35.4 0.0 copy-done.12
  35.4 0.6 dynamic-slice
  36.6 0.0 collective-permute-done.edge_ref
  36.7 0.0 copy-start.8
  36.7 0.6 collective-permute-start.2
  37.3 0.0 copy-done.11
  37.3 0.2 add_dynamic-update-slice_fusion
  37.5 13.3 %all-reduce = s32[20]{0:T(128)S(1)} all-reduce(s32[20]{0:T(128)S(1)} %add_dynamic-update-slice_fusion), channel_id=2, replica_groups=mesh['z'=8,'x'=4,'c'=2,'y'=4] {'x'}, use_global_device_ids=true, to_apply=%add | all-reduce | flops 20 | bytes 160
  50.7 0.1 reshape.24
  50.8 0.7 slice_reduce_fusion.count_ref
  51.5 0.0 all-to-all-done
  51.5 0.0 collective-permute-done.2.mate_edge_ref
  51.5 0.0 collective-permute-done.1.mate_ref
  51.5 0.0 copy-start.7
  51.6 0.0 copy-done.8
  51.6 0.0 copy-done.10
  51.6 0.8 copy-done.3
  52.4 0.1 copy-done.9
  52.5 0.3 copy-done.7
  52.8 38.6 %shard_map.95 = (bf16[4,768,128]{2,1,0:T(8,128)(2,1)}, bf16[12,768,128]{2,1,0:T(8,128)(2,1)}) custom-call(s32[4,4]{1,0:T(4,128)} %bitcast.28, s32[4]{0:T(128)} %slice_reduce_fusion.count_ref, bf16[4,768,128]{2,1,0:T(8,128)(2,1)} %bitcast.22, bf16[4,768,128]{2,1,0:T(8,128)(2,1)} %bitcast.21, bf16[2,768,128]{2,1,0:T(8,128)(2,1)} %copy-done.8, ...), custom_call_target="tpu_custom_call" | custom-call | tf_op jit(solution)/shard_map/pallas_call | solution.py:160
  91.4 0.0 copy-start.4
  91.4 1.5 %slice.24 = bf16[6,768,128]{2,1,0:T(8,128)(2,1)S(1)} slice(bf16[12,768,128]{2,1,0:T(8,128)(2,1)} %get-tuple-element.13), slice={[6:12], [0:768], [0:128]} | slice | bytes 2359296 | tf_op jit(solution)/shard_map/slice | solution.py:211
  92.9 0.1 collective-permute-start.3
  93.0 2.8 %collective-permute-done.3 = bf16[6,768,128]{2,1,0:T(8,128)(2,1)S(1)} collective-permute-done((bf16[6,768,128]{2,1,0:T(8,128)(2,1)S(1)}, bf16[6,768,128]{2,1,0:T(8,128)(2,1)S(1)}, u32[]{:S(2)}, u32[]{:S(2)}) %collective-permute-start.3) | collective-permute-done | bytes 1179680 | tf_op jit(solution)/shard_map/ppermute | solution.py:211
  95.8 1.0 copy-done.5
  96.9 0.0 copy-done.4
  96.9 0.9 add_convert_fusion.1
  97.7 4.9 %collective-permute-start.4 = (bf16[2,768,128]{2,1,0:T(8,128)(2,1)}, bf16[2,768,128]{2,1,0:T(8,128)(2,1)S(1)}, u32[]{:S(2)}, u32[]{:S(2)}) collective-permute-start(bf16[2,768,128]{2,1,0:T(8,128)(2,1)} %add_convert_fusion.1), channel_id=1, source_target_pairs={{0,32},{32,0},{64,96},{96,64},{128,160},{160,128},{192,224},{224,1... | collective-permute-start | bytes 1179656 | tf_op jit(solution)/shard_map/ppermute | solution.py:213
  102.6 4.6 %all-to-all-start.2 = ((bf16[16,192,128]{2,1,0:T(8,128)(2,1)}), bf16[16,192,128]{2,1,0:T(8,128)(2,1)S(1)}, u32[]{:S(2)}, u32[]{:S(2)}) async-start(bf16[16,192,128]{2,1,0:T(8,128)(2,1)} %bitcast.23), calls=%async_computation.2 | async-start | bytes 1572864 | tf_op jit(solution)/shard_map/all_to_all | solution.py:209
  107.2 0.0 copy-start.6
  107.2 5.0 %collective-permute-done.4 = bf16[2,768,128]{2,1,0:T(8,128)(2,1)S(1)} collective-permute-done((bf16[2,768,128]{2,1,0:T(8,128)(2,1)}, bf16[2,768,128]{2,1,0:T(8,128)(2,1)S(1)}, u32[]{:S(2)}, u32[]{:S(2)}) %collective-permute-start.4) | collective-permute-done | bytes 393248 | tf_op jit(solution)/shard_map/ppermute | solution.py:213
  112.2 0.1 broadcast_select_fusion.1
  112.3 0.0 copy-done.6
  112.3 1.2 add_convert_fusion
  113.5 8.1 %all-to-all-done.2.in_ref = bf16[16,192,128]{2,1,0:T(8,128)(2,1)S(1)} async-done(((bf16[16,192,128]{2,1,0:T(8,128)(2,1)}), bf16[16,192,128]{2,1,0:T(8,128)(2,1)S(1)}, u32[]{:S(2)}, u32[]{:S(2)}) %all-to-all-start.2) | async-done | bytes 786464 | tf_op jit(solution)/shard_map/all_to_all | solution.py:209
  121.6 3.6 %all-to-all-start.3 = ((bf16[16,192,128]{2,1,0:T(8,128)(2,1)}), bf16[16,192,128]{2,1,0:T(8,128)(2,1)S(1)}, u32[]{:S(2)}, u32[]{:S(2)}) async-start(bf16[16,192,128]{2,1,0:T(8,128)(2,1)} %bitcast.12), calls=%async_computation.3 | async-start | bytes 1572864 | tf_op jit(solution)/shard_map/all_to_all | solution.py:220
  125.3 3.5 %shard_map.96 = (bf16[192,1024]{1,0:T(8,128)(2,1)}, bf16[192,1024]{1,0:T(8,128)(2,1)}) custom-call(bf16[16,192,128]{2,1,0:T(8,128)(2,1)} %copy-done.1), custom_call_target="tpu_custom_call" | custom-call | tf_op jit(solution)/shard_map/pallas_call | solution.py:51
  128.8 9.5 %all-to-all-done.3.in_ref = bf16[16,192,128]{2,1,0:T(8,128)(2,1)S(1)} async-done(((bf16[16,192,128]{2,1,0:T(8,128)(2,1)}), bf16[16,192,128]{2,1,0:T(8,128)(2,1)S(1)}, u32[]{:S(2)}, u32[]{:S(2)}) %all-to-all-start.3) | async-done | bytes 786464 | tf_op jit(solution)/shard_map/all_to_all | solution.py:220
  138.2 0.9 copy-done.2
  139.1 3.5 %shard_map.97 = (bf16[192,1024]{1,0:T(8,128)(2,1)}, bf16[192,1024]{1,0:T(8,128)(2,1)}) custom-call(bf16[16,192,128]{2,1,0:T(8,128)(2,1)} %copy-done.2), custom_call_target="tpu_custom_call" | custom-call | tf_op jit(solution)/shard_map/pallas_call | solution.py:51
  (13 shorter events, 0.1 us)
Async XLA Ops:
  4.1 21.4 %all-to-all-start.1 = ((bf16[16,192,128]{2,1,0:T(8,128)(2,1)}), bf16[16,192,128]{2,1,0:T(8,128)(2,1)S(1)}, u32[]{:S(2)}, u32[]{:S(2)}) async-start(bf16[16,192,128]{2,1,0:T(8,128)(2,1)} %shard_map.94), calls=%async_computation.1 | async-start | bytes 1572864 | tf_op jit(solution)/shard_map/all_to_all | solution.py:199
  25.5 5.6 %copy-start = (bf16[16,192,128]{2,1,0:T(8,128)(2,1)}, bf16[16,192,128]{2,1,0:T(8,128)(2,1)S(1)}, u32[]{:S(2)}) copy-start(bf16[16,192,128]{2,1,0:T(8,128)(2,1)S(1)} %all-to-all-done.1) | copy-start | bytes 2359300
  25.6 11.1 %collective-permute-start = (bf16[2,768,128]{2,1,0:T(8,128)(2,1)S(1)}, bf16[2,768,128]{2,1,0:T(8,128)(2,1)S(1)}, u32[]{:S(2)}, u32[]{:S(2)}) collective-permute-start(bf16[2,768,128]{2,1,0:T(8,128)(2,1)S(1)} %constant_dynamic-slice_fusion), channel_id=1, source_target_pairs={{0,32},{32,0},{64,96},{96,64},{128,160},{160,128},{192,224},{224,1... | collective-permute-start | bytes 1179656 | tf_op jit(solution)/shard_map/ppermute | solution.py:205
  27.6 24.0 %collective-permute-start.1 = (bf16[4,768,128]{2,1,0:T(8,128)(2,1)S(1)}, bf16[4,768,128]{2,1,0:T(8,128)(2,1)S(1)}, u32[]{:S(2)}, u32[]{:S(2)}) collective-permute-start(bf16[4,768,128]{2,1,0:T(8,128)(2,1)S(1)} %bitcast.20), channel_id=1, source_target_pairs={{0,4},{4,0},{1,5},{5,1},{2,6},{6,2},{3,7},{7,3},{8,12},{12,8},{9,1... | collective-permute-start | bytes 2359304 | tf_op jit(solution)/shard_map/ppermute | solution.py:206
  27.6 7.8 %copy-start.12 = (u32[256]{0:T(256)S(1)}, u32[256]{0:T(256)}, u32[]{:S(2)}) copy-start(u32[256]{0:T(256)} %constant.103) | copy-start | bytes 3076
  27.6 9.7 %copy-start.11 = (s32[1,3]{1,0:T(1,128)S(1)}, s32[1,3]{1,0:T(1,128)}, u32[]{:S(2)}) copy-start(s32[1,3]{1,0:T(1,128)} %param.10) | copy-start | bytes 40
  31.1 20.4 %all-to-all-start = ((bf16[16,192,128]{2,1,0:T(8,128)(2,1)}), bf16[16,192,128]{2,1,0:T(8,128)(2,1)S(1)}, u32[]{:S(2)}, u32[]{:S(2)}) async-start(bf16[16,192,128]{2,1,0:T(8,128)(2,1)} %shard_map.93), calls=%async_computation | async-start | bytes 1572864 | tf_op jit(solution)/shard_map/all_to_all | solution.py:200
  36.7 14.9 %copy-start.8 = (bf16[2,768,128]{2,1,0:T(8,128)(2,1)}, bf16[2,768,128]{2,1,0:T(8,128)(2,1)S(1)}, u32[]{:S(2)}) copy-start(bf16[2,768,128]{2,1,0:T(8,128)(2,1)S(1)} %collective-permute-done.edge_ref) | copy-start | bytes 1179652
  36.7 14.9 %collective-permute-start.2 = (bf16[2,768,128]{2,1,0:T(8,128)(2,1)S(1)}, bf16[2,768,128]{2,1,0:T(8,128)(2,1)S(1)}, u32[]{:S(2)}, u32[]{:S(2)}) collective-permute-start(bf16[2,768,128]{2,1,0:T(8,128)(2,1)S(1)} %collective-permute-done.edge_ref), channel_id=1, source_target_pairs={{0,4},{4,0},{1,5},{5,1},{2,6},{6,2},{3,7},{7,3},{8,12},{12,8},{9,1... | collective-permute-start | bytes 1179656 | tf_op jit(solution)/shard_map/ppermute | solution.py:207
  50.8 0.7 copy-start.10
  51.5 0.9 copy-start.3
  51.5 1.0 copy-start.9
  51.5 1.3 copy-start.7
  91.4 5.5 %copy-start.4 = (bf16[12,768,128]{2,1,0:T(8,128)(2,1)S(1)}, bf16[12,768,128]{2,1,0:T(8,128)(2,1)}, u32[]{:S(2)}) copy-start(bf16[12,768,128]{2,1,0:T(8,128)(2,1)} %get-tuple-element.13) | copy-start | bytes 7077892
  92.9 2.9 %collective-permute-start.3 = (bf16[6,768,128]{2,1,0:T(8,128)(2,1)S(1)}, bf16[6,768,128]{2,1,0:T(8,128)(2,1)S(1)}, u32[]{:S(2)}, u32[]{:S(2)}) collective-permute-start(bf16[6,768,128]{2,1,0:T(8,128)(2,1)S(1)} %slice.24), channel_id=1, source_target_pairs={{0,4},{4,0},{1,5},{5,1},{2,6},{6,2},{3,7},{7,3},{8,12},{12,8},{9,1... | collective-permute-start | bytes 3538952 | tf_op jit(solution)/shard_map/ppermute | solution.py:211
  95.8 1.0 copy-start.5
  97.7 14.5 %collective-permute-start.4 = (bf16[2,768,128]{2,1,0:T(8,128)(2,1)}, bf16[2,768,128]{2,1,0:T(8,128)(2,1)S(1)}, u32[]{:S(2)}, u32[]{:S(2)}) collective-permute-start(bf16[2,768,128]{2,1,0:T(8,128)(2,1)} %add_convert_fusion.1), channel_id=1, source_target_pairs={{0,32},{32,0},{64,96},{96,64},{128,160},{160,128},{192,224},{224,1... | collective-permute-start | bytes 1179656 | tf_op jit(solution)/shard_map/ppermute | solution.py:213
  102.6 19.0 %all-to-all-start.2 = ((bf16[16,192,128]{2,1,0:T(8,128)(2,1)}), bf16[16,192,128]{2,1,0:T(8,128)(2,1)S(1)}, u32[]{:S(2)}, u32[]{:S(2)}) async-start(bf16[16,192,128]{2,1,0:T(8,128)(2,1)} %bitcast.23), calls=%async_computation.2 | async-start | bytes 1572864 | tf_op jit(solution)/shard_map/all_to_all | solution.py:209
  107.2 5.0 %copy-start.6 = (bf16[6,768,128]{2,1,0:T(8,128)(2,1)S(1)}, bf16[6,768,128]{2,1,0:T(8,128)(2,1)}, u32[]{:S(2)}) copy-start(bf16[6,768,128]{2,1,0:T(8,128)(2,1)} %copy-done.5) | copy-start | bytes 3538948
  121.6 3.6 %copy-start.1 = (bf16[16,192,128]{2,1,0:T(8,128)(2,1)}, bf16[16,192,128]{2,1,0:T(8,128)(2,1)S(1)}, u32[]{:S(2)}) copy-start(bf16[16,192,128]{2,1,0:T(8,128)(2,1)S(1)} %all-to-all-done.2.in_ref) | copy-start | bytes 2359300
  121.6 16.6 %all-to-all-start.3 = ((bf16[16,192,128]{2,1,0:T(8,128)(2,1)}), bf16[16,192,128]{2,1,0:T(8,128)(2,1)S(1)}, u32[]{:S(2)}, u32[]{:S(2)}) async-start(bf16[16,192,128]{2,1,0:T(8,128)(2,1)} %bitcast.12), calls=%async_computation.3 | async-start | bytes 1572864 | tf_op jit(solution)/shard_map/all_to_all | solution.py:220
  138.2 0.9 copy-start.2
where the time goes:
time: 144 us; the launch traced here: 143 us
  Pallas kernels  52.6 us (37%)
  waiting for transfers between devices  39.7 us (28%)
  starting transfers between devices  26.5 us (18%)
  blocking collectives  13.3 us (9%)
  local copies, waits for them, and re-layouts  6.07 us (4%)
  other arithmetic  2.34 us (2%)
  between operations  2.14 us (1%)
    pallas_call x1, Pallas kernels, attention(): pl.pallas_call(attention_kernel, in_specs=[smem, smem, vmem, hbm, hbm, hb...  38.6 us
    all_to_all x1, waiting for transfers between devices, local(): lax.all_to_all(kv, ('x', 'y'), 0, 0, tiled=True).reshape(ROW, TOK, PAIR)  14.3 us
    unnamed x1, blocking collectives  13.3 us
    all_to_all x1, waiting for transfers between devices, local(): lax.all_to_all(dkv_sum.reshape(HEADS, PIECE, PAIR), ('x', 'y'), 0, 0, til...  9.45 us
    all_to_all x1, waiting for transfers between devices, local(): lax.all_to_all(od.reshape(HEADS, PIECE, PAIR), ('x', 'y'), 0, 0, tiled=True)  8.12 us
    pallas_call x2, Pallas kernels, pack(): pl.pallas_call(pack_kernel, grid=(steps,), in_specs=[pl.BlockSpec((PIECE,...  7.04 us
    all_to_all x1, starting transfers between devices, local(): lax.all_to_all(kv, ('x', 'y'), 0, 0, tiled=True).reshape(ROW, TOK, PAIR)  7.03 us
    pallas_call x2, Pallas kernels, unpack(): pl.pallas_call(unpack_kernel, grid=(steps,), in_specs=[pl.BlockSpec((HEAD...  7.03 us
  transfers between devices with their start and end apart: 9, of which 5 were waited for; matrix products, arithmetic and copies ran while one was open for 2% of the time, Pallas kernels for 5%

commit v1 on v0

v1 whole, which is shorter than its diff:
```python
import jax
import jax.numpy as jnp
from jax import lax
from jax.experimental import pallas as pl
from jax.experimental.pallas import tpu as pltpu
from jax.sharding import Mesh, PartitionSpec as P

HEAD_DIM = 64
PAIR = 2 * HEAD_DIM
HEADS = 16
WIDTH = HEADS * HEAD_DIM
TOK = 768
PIECE = 192
QUARTERS = TOK // PIECE
ROW = 4
EDGE = 2
NEAR = 2 * ROW
MAXNB = 3
SLOTS = 1 + MAXNB
SUMS = HEAD_DIM + 16
TOP = HEAD_DIM + 8
CODES = 32
NEAR_COUNT = CODES - 2
EDGE_COUNT = CODES - 1
KERNEL_MIB = 48
EDGE_MIB = 48
SCALE = HEAD_DIM ** (-0.5)
BF = jnp.bfloat16
F32 = jnp.float32

ANY = pl.BlockSpec(memory_space=pl.ANY)
HBM = pl.BlockSpec(memory_space=pltpu.HBM)
SMEM = pl.BlockSpec(memory_space=pltpu.SMEM)
VMEM = pl.BlockSpec(memory_space=pltpu.VMEM)


def params(mib):
    return pltpu.CompilerParams(vmem_limit_bytes=mib * 1024 * 1024)


def shape(dims, dtype=BF):
    return jax.ShapeDtypeStruct(dims, dtype)


def cost(flops, moved):
    return pl.CostEstimate(flops=flops, bytes_accessed=moved, transcendentals=0)


def block(*lead):
    return lead + (QUARTERS, PIECE, PAIR)


def pack_kernel(q_ref, k_ref, v_ref, g_ref, out_ref):
    for side, (a, b) in enumerate(((k_ref, v_ref), (q_ref, g_ref))):
        for h in range(HEADS):
            cols = slice(h * HEAD_DIM, (h + 1) * HEAD_DIM)
            out_ref[h, side] = jnp.concatenate([a[:, cols], b[:, cols]], axis=1)


def pack(*arrays):
    return pl.pallas_call(
        pack_kernel,
        in_specs=[VMEM] * 4,
        out_specs=VMEM,
        out_shape=shape((HEADS, 2, PIECE, PAIR)),
        compiler_params=params(60),
    )(*arrays)


def unpack_kernel(in_ref, a_ref, q_ref, k_ref, v_ref):
    for side, (a, b) in enumerate(((k_ref, v_ref), (a_ref, q_ref))):
        for h in range(HEADS):
            cols = slice(h * HEAD_DIM, (h + 1) * HEAD_DIM)
            a[:, cols] = in_ref[h, side, :, :HEAD_DIM]
            b[:, cols] = in_ref[h, side, :, HEAD_DIM:]


def unpack(packed):
    return pl.pallas_call(
        unpack_kernel,
        in_specs=[VMEM],
        out_specs=[VMEM] * 4,
        out_shape=[shape((PIECE, WIDTH))] * 4,
        compiler_params=params(16),
    )(packed)


def dot(a, b):
    return jnp.dot(a, b, preferred_element_type=F32)


def dot_nt(a, b):
    return lax.dot_general(a, b, (((1,), (1,)), ((), ())), preferred_element_type=F32)


def flat(ref):
    return ref[...].reshape(TOK, PAIR)


def low_lanes():
    return lax.broadcasted_iota(jnp.int32, (TOK, PAIR), 1) < HEAD_DIM


def query_side(qg):
    return jnp.where(low_lanes(), qg * SCALE, jnp.zeros_like(qg)).astype(BF)


def scores_of(kv, q_side):
    scores = dot_nt(kv, q_side)
    return scores, jnp.max(scores, axis=0, keepdims=True)


def values_of(kv, scores, top):
    e = jnp.exp(scores - top).astype(BF)
    left = jnp.concatenate([kv.T[HEAD_DIM:], jnp.ones((16, TOK), BF)], axis=0)
    part = dot(left, e)
    return e, jnp.concatenate([part[:TOP], jnp.broadcast_to(top, (8, TOK))], axis=0)


def grad_rows(qg_t, delta):
    d_hi = delta.astype(BF)
    rest = delta - d_hi.astype(F32)
    d_mid = rest.astype(BF)
    d_lo = (rest - d_mid.astype(F32)).astype(BF)
    sub = lax.broadcasted_iota(jnp.int32, (PAIR, TOK), 0)
    low = jnp.where(sub == 0, -d_hi, jnp.where(sub == 1, -d_mid, jnp.where(sub == 2, -d_lo, jnp.zeros_like(qg_t))))
    return jnp.where(sub < HEAD_DIM, low, qg_t)


def backward_pair(kv, e, share, g_t, q_side, g_side):
    dprobs = dot(jnp.where(low_lanes(), jnp.ones_like(kv), kv), g_t)
    p = e.astype(F32) * share
    ds = (p * dprobs).astype(BF)
    dq = dot(kv.T[:HEAD_DIM], ds)
    return dq, dot(ds, q_side) + dot(p.astype(BF), g_side)


def decode(codes, n):
    code = codes[n]
    return code >> 6, (code >> 4) & 3, code & 15


def list_pairs(x, rows, codes):
    n = jnp.int32(0)
    for kind in range(2):
        for t in range(ROW):
            view = (x + t) & (ROW - 1)
            for b in range(SLOTS):
                place = rows[t, b]
                codes[n] = view * 64 + b * 16 + place
                wanted = place < NEAR if kind == 0 else place >= NEAR
                n = n + jnp.where(jnp.logical_and(b < rows[t, SLOTS], wanted), 1, 0)
        if kind == 0:
            near = n
    codes[NEAR_COUNT] = near
    codes[EDGE_COUNT] = n - near


def merge(acc, j, part, top):
    old_top = acc[j, TOP : TOP + 1]
    new_top = jnp.maximum(old_top, top)
    acc[j, :TOP] = acc[j, :TOP] * jnp.exp(old_top - new_top) + part[:TOP] * jnp.exp(top - new_top)
    acc[j, TOP:] = jnp.broadcast_to(new_top, (8, TOK))


def forward_near_kernel(
    x_ref, rows, arrived, mate, e_out, acc_out, tops_out, codes,
    kv, qg, q_side, scores, top_now, e, acc, tops, sems, e_sems, out_sems,
):
    loads = []
    for x in range(ROW):
        loads.append(pltpu.make_async_copy(arrived.at[x, :, 1], qg.at[x], sems.at[x]))
        loads.append(pltpu.make_async_copy(arrived.at[x, :, 0], kv.at[x], sems.at[ROW + x]))
    loads.append(pltpu.make_async_copy(mate, kv.at[ROW:NEAR], sems.at[2 * ROW]))
    for load in loads:
        load.start()
    list_pairs(x_ref[0], rows, codes)
    acc[...] = jnp.zeros_like(acc)
    for x in range(ROW):
        acc[x, TOP:] = jnp.full((8, TOK), -jnp.inf, F32)
    for load in loads:
        load.wait()
    for x in range(ROW):
        q_side[x] = query_side(flat(qg.at[x]))

    def store(j, b, ring):
        return pltpu.make_async_copy(e.at[ring], e_out.at[j, b], e_sems.at[ring])

    def score(n, ring):
        j, _, i = decode(codes, n)
        scores[ring], top_now[ring] = scores_of(flat(kv.at[i]), q_side[j])

    count = codes[NEAR_COUNT]
    score(0, 0)

    def one_pair(n, carry):
        ring = n % 2
        j, b, i = decode(codes, n)

        @pl.when(n >= 2)
        def _():
            store(j, b, ring).wait()

        top = top_now[ring]
        e[ring], part = values_of(flat(kv.at[i]), scores[ring], top)
        score(jnp.minimum(n + 1, count - 1), 1 - ring)
        merge(acc, j, part, top)
        tops[j, pl.ds(b, 1), :] = top
        store(j, b, ring).start()
        return carry

    lax.fori_loop(0, count, one_pair, 0)
    outs = [
        pltpu.make_async_copy(acc, acc_out, out_sems.at[0]),
        pltpu.make_async_copy(tops, tops_out, out_sems.at[1]),
    ]
    for out in outs:
        out.start()
    for ring in range(2):
        store(0, 0, ring).wait()
    for out in outs:
        out.wait()


def forward_near(x, rows, arrived, mate):
    return pl.pallas_call(
        forward_near_kernel,
        in_specs=[SMEM] * 2 + [ANY] * 2,
        out_specs=[HBM, ANY, ANY, SMEM],
        out_shape=[
            shape((ROW, SLOTS, TOK, TOK)),
            shape((ROW, SUMS, TOK), F32),
            shape((ROW, 8, TOK), F32),
            shape((CODES,), jnp.int32),
        ],
        scratch_shapes=[
            pltpu.VMEM(block(NEAR), BF),
            pltpu.VMEM(block(ROW), BF),
            pltpu.VMEM((ROW, TOK, PAIR), BF),
            pltpu.VMEM((2, TOK, TOK), F32),
            pltpu.VMEM((2, 1, TOK), F32),
            pltpu.VMEM((2, TOK, TOK), BF),
            pltpu.VMEM((ROW, SUMS, TOK), F32),
            pltpu.VMEM((ROW, 8, TOK), F32),
            pltpu.SemaphoreType.DMA((2 * ROW + 1,)),
            pltpu.SemaphoreType.DMA((2,)),
            pltpu.SemaphoreType.DMA((2,)),
        ],
        compiler_params=params(KERNEL_MIB),
        cost_estimate=cost(9 * 10**9, 20 * 10**6),
    )(x, rows, arrived, mate)


def edge_kernel(
    codes, arrived, edge, mate_edge, acc_in, tops_in,
    att_out, dq_out, shares_out, g_t_out, d_edge, d_mate_edge,
    kv, qg, acc, tops, e, scores, top_now, total, dq_sum, q_side, g_side, g_t, att, shares, d_out, sems, out_sems,
):
    loads = []
    for x in range(ROW):
        loads.append(pltpu.make_async_copy(arrived.at[x, :, 1], qg.at[x], sems.at[x]))
    loads.append(pltpu.make_async_copy(edge, kv.at[0:EDGE], sems.at[ROW]))
    loads.append(pltpu.make_async_copy(mate_edge, kv.at[EDGE : 2 * EDGE], sems.at[ROW + 1]))
    loads.append(pltpu.make_async_copy(acc_in, acc, sems.at[ROW + 2]))
    loads.append(pltpu.make_async_copy(tops_in, tops, sems.at[ROW + 3]))
    for load in loads:
        load.start()
    total[...] = jnp.zeros_like(total)
    dq_sum[...] = jnp.zeros_like(dq_sum)
    for load in loads:
        load.wait()
    for x in range(ROW):
        qg_now = flat(qg.at[x])
        q_side[x] = query_side(qg_now)
        g_side[x] = jnp.where(low_lanes(), jnp.zeros_like(qg_now), qg_now)

    first, count = codes[NEAR_COUNT], codes[EDGE_COUNT]

    def score(n, ring):
        j, _, i = decode(codes, first + n)
        scores[ring], top_now[ring] = scores_of(flat(kv.at[i - NEAR]), q_side[j])

    @pl.when(count > 0)
    def _():
        score(0, 0)

    def one_forward(n, carry):
        ring = n % 2
        j, b, i = decode(codes, first + n)
        top = top_now[ring]
        e[n], part = values_of(flat(kv.at[i - NEAR]), scores[ring], top)
        score(jnp.minimum(n + 1, count - 1), 1 - ring)
        merge(acc, j, part, top)
        tops[j, pl.ds(b, 1), :] = top
        return carry

    lax.fori_loop(0, count, one_forward, 0)

    for j in range(ROW):
        inverse = 1.0 / acc[j, HEAD_DIM : HEAD_DIM + 1]
        att_now = acc[j, :HEAD_DIM] * inverse
        qg_t = flat(qg.at[j]).T
        delta = jnp.sum(qg_t[HEAD_DIM:].astype(F32) * att_now, axis=0, keepdims=True)
        att[j] = att_now.astype(BF)
        shares[j] = jnp.exp(tops[j] - acc[j, TOP : TOP + 1]) * inverse
        g_t[j] = grad_rows(qg_t, delta)

    early = [
        pltpu.make_async_copy(att, att_out, out_sems.at[0]),
        pltpu.make_async_copy(shares, shares_out, out_sems.at[1]),
        pltpu.make_async_copy(g_t, g_t_out, out_sems.at[2]),
    ]
    for out in early:
        out.start()

    def one_backward(n, carry):
        j, b, i = decode(codes, first + n)
        share = shares[j, pl.ds(b, 1), :]
        dq, terms = backward_pair(flat(kv.at[i - NEAR]), e[n], share, g_t[j], q_side[j], g_side[j])
        total[i - NEAR] += terms
        dq_sum[j] += dq
        return carry

    lax.fori_loop(0, count, one_backward, 0)
    for i in range(2 * EDGE):
        d_out[i] = total[i].astype(BF).reshape(QUARTERS, PIECE, PAIR)
    late = [
        pltpu.make_async_copy(d_out.at[0:EDGE], d_edge, out_sems.at[3]),
        pltpu.make_async_copy(d_out.at[EDGE : 2 * EDGE], d_mate_edge, out_sems.at[4]),
        pltpu.make_async_copy(dq_sum, dq_out, out_sems.at[5]),
    ]
    for out in late:
        out.start()
    for out in early + late:
        out.wait()


def edges(codes, arrived, edge, mate_edge, acc, tops):
    return pl.pallas_call(
        edge_kernel,
        in_specs=[SMEM] + [ANY] * 5,
        out_specs=[ANY] * 6,
        out_shape=[
            shape((ROW, HEAD_DIM, TOK)),
            shape((ROW, HEAD_DIM, TOK), F32),
            shape((ROW, 8, TOK), F32),
            shape((ROW, PAIR, TOK)),
            shape(block(EDGE)),
            shape(block(EDGE)),
        ],
        scratch_shapes=[
            pltpu.VMEM(block(2 * EDGE), BF),
            pltpu.VMEM(block(ROW), BF),
            pltpu.VMEM((ROW, SUMS, TOK), F32),
            pltpu.VMEM((ROW, 8, TOK), F32),
            pltpu.VMEM((ROW * MAXNB, TOK, TOK), BF),
            pltpu.VMEM((2, TOK, TOK), F32),
            pltpu.VMEM((2, 1, TOK), F32),
            pltpu.VMEM((2 * EDGE, TOK, PAIR), F32),
            pltpu.VMEM((ROW, HEAD_DIM, TOK), F32),
            pltpu.VMEM((ROW, TOK, PAIR), BF),
            pltpu.VMEM((ROW, TOK, PAIR), BF),
            pltpu.VMEM((ROW, PAIR, TOK), BF),
            pltpu.VMEM((ROW, HEAD_DIM, TOK), BF),
            pltpu.VMEM((ROW, 8, TOK), F32),
            pltpu.VMEM(block(2 * EDGE), BF),
            pltpu.SemaphoreType.DMA((ROW + 4,)),
            pltpu.SemaphoreType.DMA((6,)),
        ],
        compiler_params=params(EDGE_MIB),
        cost_estimate=cost(9 * 10**9, 10 * 10**6),
    )(codes, arrived, edge, mate_edge, acc, tops)


def backward_near_kernel(
    codes, arrived, mate, e_in, att_in, dq_in, shares_in, g_t_in, edge_sum,
    od_out, d_own, d_mate,
    kv, qg, e, total, dq_sum, q_side, g_side, g_t, att, shares, od, d_out, sems, e_sems, out_sems,
):
    loads = []
    for x in range(ROW):
        loads.append(pltpu.make_async_copy(arrived.at[x, :, 1], qg.at[x], sems.at[x]))
        loads.append(pltpu.make_async_copy(arrived.at[x, :, 0], kv.at[x], sems.at[ROW + x]))
    loads.append(pltpu.make_async_copy(mate, kv.at[ROW:NEAR], sems.at[2 * ROW]))
    loads.append(pltpu.make_async_copy(g_t_in, g_t, sems.at[2 * ROW + 1]))
    loads.append(pltpu.make_async_copy(shares_in, shares, sems.at[2 * ROW + 2]))
    later = [
        pltpu.make_async_copy(dq_in, dq_sum, sems.at[2 * ROW + 3]),
        pltpu.make_async_copy(att_in, att, sems.at[2 * ROW + 4]),
    ]

    def fetch(n, ring):
        j, b, _ = decode(codes, n)
        return pltpu.make_async_copy(e_in.at[j, b], e.at[ring], e_sems.at[ring])

    count = codes[NEAR_COUNT]
    fetch(0, 0).start()
    for load in loads + later:
        load.start()
    total[...] = jnp.zeros_like(total)
    for load in loads:
        load.wait()
    for x in range(ROW):
        qg_now = flat(qg.at[x])
        q_side[x] = query_side(qg_now)
        g_side[x] = jnp.where(low_lanes(), jnp.zeros_like(qg_now), qg_now)
    for load in later:
        load.wait()

    def one_pair(n, carry):
        ring = n % 2
        j, b, i = decode(codes, n)
        fetch(n, ring).wait()

        @pl.when(n + 1 < count)
        def _():
            fetch(n + 1, 1 - ring).start()

        share = shares[j, pl.ds(b, 1), :]
        dq, terms = backward_pair(flat(kv.at[i]), e[ring], share, g_t[j], q_side[j], g_side[j])
        total[i] += terms
        dq_sum[j] += dq
        return carry

    lax.fori_loop(0, count, one_pair, 0)
    outs = [
        pltpu.make_async_copy(d_out.at[ROW:NEAR], d_mate, out_sems.at[ROW]),
        pltpu.make_async_copy(d_out.at[0:ROW], d_own, out_sems.at[ROW + 1]),
    ]
    for x in range(ROW):
        outs.append(pltpu.make_async_copy(od.at[x], od_out.at[x], out_sems.at[x]))
    for i in range(ROW):
        d_out[ROW + i] = total[ROW + i].astype(BF).reshape(QUARTERS, PIECE, PAIR)
    outs[0].start()
    for i in range(ROW):
        d_out[i] = total[i].astype(BF).reshape(QUARTERS, PIECE, PAIR)
    outs[1].start()
    for x in range(ROW):
        both = jnp.concatenate([att[x], (dq_sum[x] * SCALE).astype(BF)], axis=0)
        od[x] = both.T.reshape(QUARTERS, PIECE, PAIR)
        outs[2 + x].start()
    for store in outs:
        store.wait()


def backward_near(codes, arrived, mate, e, att, dq, shares, g_t, edge_sum):
    return pl.pallas_call(
        backward_near_kernel,
        in_specs=[SMEM, ANY, ANY, HBM] + [ANY] * 5,
        out_specs=[ANY] * 3,
        out_shape=[shape(block(ROW))] * 3,
        scratch_shapes=[
            pltpu.VMEM(block(NEAR), BF),
            pltpu.VMEM(block(ROW), BF),
            pltpu.VMEM((2, TOK, TOK), BF),
            pltpu.VMEM((NEAR, TOK, PAIR), F32),
            pltpu.VMEM((ROW, HEAD_DIM, TOK), F32),
            pltpu.VMEM((ROW, TOK, PAIR), BF),
            pltpu.VMEM((ROW, TOK, PAIR), BF),
            pltpu.VMEM((ROW, PAIR, TOK), BF),
            pltpu.VMEM((ROW, HEAD_DIM, TOK), BF),
            pltpu.VMEM((ROW, 8, TOK), F32),
            pltpu.VMEM(block(ROW), BF),
            pltpu.VMEM(block(NEAR), BF),
            pltpu.SemaphoreType.DMA((2 * ROW + 5,)),
            pltpu.SemaphoreType.DMA((2,)),
            pltpu.SemaphoreType.DMA((ROW + 2,)),
        ],
        compiler_params=params(KERNEL_MIB),
        cost_estimate=cost(15 * 10**9, 20 * 10**6),
    )(codes, arrived, mate, e, att, dq, shares, g_t, edge_sum)


def fold_kernel(upper, own, got, edge_got, od, out, sums, sems, od_sem):
    kept = pltpu.make_async_copy(od, out.at[:, :, 1], od_sem)
    kept.start()
    stores = []
    for x in range(ROW):
        total = own[x].astype(F32) + got[x].astype(F32)
        listed = upper[0] == (0 if x >= EDGE else 1)
        far = edge_got[x % EDGE].astype(F32)
        sums[x] = (total + jnp.where(listed, far, jnp.zeros_like(far))).astype(BF)
        stores.append(pltpu.make_async_copy(sums.at[x], out.at[x, :, 0], sems.at[x]))
        stores[x].start()
    for store in stores:
        store.wait()
    kept.wait()


def fold(upper, own, got, edge_got, od):
    return pl.pallas_call(
        fold_kernel,
        in_specs=[SMEM, VMEM, VMEM, VMEM, ANY],
        out_specs=HBM,
        out_shape=shape((ROW, QUARTERS, 2, PIECE, PAIR)),
        scratch_shapes=[
            pltpu.VMEM(block(ROW), BF),
            pltpu.SemaphoreType.DMA((ROW,)),
            pltpu.SemaphoreType.DMA,
        ],
        compiler_params=params(16),
    )(upper, own, got, edge_got, od)


def block_rows(nbr_views, nbr_counts):
    z, x, c = lax.axis_index("z"), lax.axis_index("x"), lax.axis_index("c")
    at = nbr_views[0] % (4 * ROW)
    same_row = (at // NEAR) == (z % 2)
    column = (at // 2) % ROW
    place = jnp.where(same_row, column, NEAR + column % EDGE)
    place = place + jnp.where(at % 2 == c, 0, jnp.where(same_row, ROW, EDGE))
    mine = jnp.concatenate([x[None].astype(jnp.int32), place, nbr_counts + 1]).astype(jnp.int32)
    rows = [mine]
    for by in range(1, ROW):
        rows.append(lax.ppermute(mine, "x", [(i, (i - by) % ROW) for i in range(ROW)]))
    return x[None].astype(jnp.int32), jnp.stack(rows)


def local(queries, keys, values, out_grad, nbr_views, nbr_counts):
    x, rows_of_views = block_rows(nbr_views, nbr_counts)
    cores = [(0, 1), (1, 0)]
    rows = [(i, i ^ 1) for i in range(lax.axis_size("z"))]
    upper = lax.axis_index("z") % 2
    packed = pack(queries[0], keys[0], values[0], out_grad[0])
    arrived = lax.all_to_all(packed.reshape(HEADS, 2 * PIECE, PAIR), ("x", "y"), 0, 0, tiled=True)
    arrived, rows_of_views = lax.optimization_barrier((arrived, rows_of_views))
    arrived = arrived.reshape(ROW, QUARTERS, 2, PIECE, PAIR)
    start = jnp.where(upper == 1, 0, ROW - EDGE)
    edge = lax.ppermute(lax.dynamic_slice_in_dim(arrived, start, EDGE, 0)[:, :, 0], "z", rows)
    mate = lax.ppermute(arrived[:, :, 0], "c", cores)
    e, acc, tops, codes = forward_near(x, rows_of_views, arrived, mate)
    edge, acc = lax.optimization_barrier((edge, acc))
    mate_edge = lax.ppermute(edge, "c", cores)
    att, dq, shares, g_t, d_edge, d_mate_edge = edges(codes, arrived, edge, mate_edge, acc, tops)
    edge_sum = d_edge.astype(F32) + lax.ppermute(d_mate_edge, "c", cores).astype(F32)
    edge_sum = edge_sum.astype(BF)
    edge_got = lax.ppermute(edge_sum, "z", rows)
    od, d_own, d_mate = backward_near(codes, arrived, mate, e, att, dq, shares, g_t, edge_sum)
    d_mate, edge_got = lax.optimization_barrier((d_mate, edge_got))
    got = lax.ppermute(d_mate, "c", cores)
    out = fold(upper.astype(jnp.int32)[None], d_own, got, edge_got, od)
    back = lax.all_to_all(out.reshape(HEADS, 2 * PIECE, PAIR), ("x", "y"), 0, 0, tiled=True)
    results = unpack(back.reshape(HEADS, 2, PIECE, PAIR))
    return tuple(result[None] for result in results)


def solution(mesh):
    fine = Mesh(mesh.devices.reshape(8, 4, 2, 4), ("z", "x", "c", "y"))
    views = ("z", "x", "c")
    tokens = P(views, "y", None)
    return jax.shard_map(
        local,
        mesh=fine,
        in_specs=(tokens, tokens, tokens, tokens, P(views, None), P(views)),
        out_specs=(tokens, tokens, tokens, tokens),
        check_vma=False,
    )
```

time: 144 us -> 119 us (0.83)
  waiting for transfers between devices: 39.7 us -> 23 us
  blocking collectives: 13.3 us -> 26.8 us
  starting transfers between devices: 26.5 us -> 19.7 us
  local copies, waits for them, and re-layouts: 6.07 us -> 0.09 us
  Pallas kernels: 52.6 us -> 46.8 us
  other arithmetic: 2.34 us -> 0.31 us
    all_to_all x4 -> x1, waiting for transfers between devices: 31.9 us -> 3.11 us  [local(): lax.all_to_all(packed.reshape(HEADS, 2 * PIECE, PAIR), ('x', 'y'), 0, 0,...]
    all_to_all x0 -> x1, blocking collectives: none -> 26.8 us  [local(): lax.all_to_all(out.reshape(HEADS, 2 * PIECE, PAIR), ('x', 'y'), 0, 0, til...]
    ppermute x3 -> x7, waiting for transfers between devices: 2.84 us -> 18.2 us  [the longest x3 14.3 us: block_rows(): lax.ppermute(mine, 'x', [(i, (i - by) % ROW) for i in range(ROW)])]
    unnamed x1 -> x0, blocking collectives: 13.3 us -> none
    all_to_all x4 -> x1, starting transfers between devices: 18.9 us -> 7.17 us  [local(): lax.all_to_all(packed.reshape(HEADS, 2 * PIECE, PAIR), ('x', 'y'), 0, 0,...]
    ppermute x3 -> x7, starting transfers between devices: 2.1 us -> 10.5 us  [the longest x3 5.48 us: block_rows(): lax.ppermute(mine, 'x', [(i, (i - by) % ROW) for i in range(ROW)])]
    pallas_call x5 -> x6, Pallas kernels: 52.6 us -> 46.8 us  [the longest x1 22.8 us: backward_near(): pl.pallas_call(backward_near_kernel, in_specs=[SMEM, ANY, ANY, HBM] + [AN...]
    ppermute x1, waiting for transfers between devices: 4.96 us -> 0.01 us  [local(): edge_got = lax.ppermute(edge_sum, 'z', rows)]
  transfers between devices with their start and end apart: 9 -> 10, of which waited for: 5 -> 6; matrix products, arithmetic and copies ran while one was open for 2% -> 0% of each run, Pallas kernels for 5% -> 32%
where the time goes in v1:
time: 119 us; the launch traced here: 118 us
  Pallas kernels  46.8 us (39%)
  blocking collectives  26.8 us (23%)
  waiting for transfers between devices  23 us (19%)
  starting transfers between devices  19.7 us (17%)
  between operations  1.43 us (1%)
    all_to_all x1, blocking collectives, local(): lax.all_to_all(out.reshape(HEADS, 2 * PIECE, PAIR), ('x', 'y'), 0, 0, til...  26.8 us
    pallas_call x1, Pallas kernels, backward_near(): pl.pallas_call(backward_near_kernel, in_specs=[SMEM, ANY, ANY, HBM] + [AN...  22.8 us
    pallas_call x1, Pallas kernels, forward_near(): pl.pallas_call(forward_near_kernel, in_specs=[SMEM] * 2 + [ANY] * 2, out_...  14.7 us
    ppermute x3, waiting for transfers between devices, block_rows(): lax.ppermute(mine, 'x', [(i, (i - by) % ROW) for i in range(ROW)])  14.3 us
    all_to_all x1, starting transfers between devices, local(): lax.all_to_all(packed.reshape(HEADS, 2 * PIECE, PAIR), ('x', 'y'), 0, 0,...  7.17 us
    ppermute x3, starting transfers between devices, block_rows(): lax.ppermute(mine, 'x', [(i, (i - by) % ROW) for i in range(ROW)])  5.48 us
    pallas_call x1, Pallas kernels, edges(): pl.pallas_call(edge_kernel, in_specs=[SMEM] + [ANY] * 5, out_specs=[ANY]...  3.47 us
    all_to_all x1, waiting for transfers between devices, local(): lax.all_to_all(packed.reshape(HEADS, 2 * PIECE, PAIR), ('x', 'y'), 0, 0,...  3.11 us
  transfers between devices with their start and end apart: 10, of which 6 were waited for; matrix products, arithmetic and copies ran while one was open for 0% of the time, Pallas kernels for 32%

profile of v1, /device:TPU:64, one launch (start us, length us, event | category | flops | bytes accessed | tf_op | source)
XLA Modules:
  0.0 118.1 jit_solution(9620044158116679727)
XLA Ops:
  0.6 3.0 %shard_map.93 = bf16[16,2,192,128]{3,2,1,0:T(8,128)(2,1)} custom-call(bf16[192,1024]{1,0:T(8,128)(2,1)} %bitcast.39, bf16[192,1024]{1,0:T(8,128)(2,1)} %bitcast.40, bf16[192,1024]{1,0:T(8,128)(2,1)} %bitcast.41, bf16[192,1024]{1,0:T(8,128)(2,1)} %bitcast.42), custom_call_target="tpu_custom_call" | custom-call | tf_op jit(solution)/shard_map/pallas_call | solution.py:61
  3.6 0.0 copy-start.1
  3.6 7.2 %all-to-all-start = ((bf16[16,384,128]{2,1,0:T(8,128)(2,1)}), bf16[16,384,128]{2,1,0:T(8,128)(2,1)S(1)}, u32[]{:S(2)}, u32[]{:S(2)}) async-start(bf16[16,384,128]{2,1,0:T(8,128)(2,1)} %bitcast.38), calls=%async_computation | async-start | bytes 3145728 | tf_op jit(solution)/shard_map/all_to_all | solution.py:525
  11.5 0.0 copy-done.1
  11.5 0.1 pad_add_fusion.1
  11.6 3.5 %collective-permute-start.1 = (s32[5]{0:T(128)S(1)}, s32[5]{0:T(128)S(1)}, u32[]{:S(2)}, u32[]{:S(2)}) collective-permute-start(s32[5]{0:T(128)S(1)} %pad_add_fusion.1), channel_id=1, source_target_pairs={{0,16},{8,24},{16,0},{24,8},{1,17},{9,25},{17,1},{25,9},{2,18},{10... | collective-permute-start | bytes 68 | tf_op jit(solution)/shard_map/ppermute | solution.py:515
  15.1 1.2 collective-permute-start
  16.2 0.9 collective-permute-start.2
  17.1 0.1 fusion.5
  17.2 14.3 %collective-permute-done.1 = s32[5]{0:T(128)S(1)} collective-permute-done((s32[5]{0:T(128)S(1)}, s32[5]{0:T(128)S(1)}, u32[]{:S(2)}, u32[]{:S(2)}) %collective-permute-start.1) | collective-permute-done | bytes 52 | tf_op jit(solution)/shard_map/ppermute | solution.py:515
  31.5 0.0 collective-permute-done
  31.5 0.0 collective-permute-done.2
  31.5 3.1 %all-to-all-done = bf16[16,384,128]{2,1,0:T(8,128)(2,1)S(1)} async-done(((bf16[16,384,128]{2,1,0:T(8,128)(2,1)}), bf16[16,384,128]{2,1,0:T(8,128)(2,1)S(1)}, u32[]{:S(2)}, u32[]{:S(2)}) %all-to-all-start) | async-done | bytes 1572896 | tf_op jit(solution)/shard_map/all_to_all | solution.py:525
  34.6 0.0 copy-start
  34.6 0.1 slice_bitcast_fusion
  34.7 0.1 collective-permute-start.3
  34.8 2.0 %collective-permute-start.4 = (bf16[2,4,192,128]{3,2,1,0:T(8,128)(2,1)S(1)}, bf16[2,4,192,128]{3,2,1,0:T(8,128)(2,1)S(1)}, u32[]{:S(2)}, u32[]{:S(2)}) collective-permute-start(bf16[2,4,192,128]{3,2,1,0:T(8,128)(2,1)S(1)} %dynamic-slice_bitcast_fusion), channel_id=1, source_target_pairs={{0,32},{32,0},{64,96},{96,64},{128,160},{160,128},{192,224},{224,1... | collective-permute-start | bytes 1179656 | tf_op jit(solution)/shard_map/ppermute | solution.py:529
  36.8 0.2 collective-permute-done.3.mate
  37.0 14.7 %shard_map.94 = (bf16[4,4,768,768]{3,2,1,0:T(8,128)(2,1)}, f32[4,80,768]{2,1,0:T(8,128)S(1)}, f32[4,8,768]{2,1,0:T(8,128)S(1)}, s32[32]{0:T(128)S(1)}) custom-call(s32[1]{0:T(128)} %bitcast.1.x_ref, s32[4,5]{1,0:T(4,128)S(1)} %pad_add_fusion.rows, bf16[4,4,2,192,128]{4,3,2,1,0:T(8,128)(2,1)S(1)} %bitcast.35, ...), custom_call_target="tpu_custom_call" | custom-call | flops 8999999488 | bytes 20000000 | tf_op jit(solution)/shard_map/pallas_call | solution.py:226
  51.8 0.0 copy-done
  51.8 0.0 collective-permute-done.4.edge
  51.8 0.1 collective-permute-start.5
  51.9 1.7 %collective-permute-done.5.mate_edge = bf16[2,4,192,128]{3,2,1,0:T(8,128)(2,1)S(1)} collective-permute-done((bf16[2,4,192,128]{3,2,1,0:T(8,128)(2,1)S(1)}, bf16[2,4,192,128]{3,2,1,0:T(8,128)(2,1)S(1)}, u32[]{:S(2)}, u32[]{:S(2)}) %collective-permute-start.5) | collective-permute-done | bytes 393248 | tf_op jit(solution)/shard_map/ppermute | solution.py:533
  53.6 3.5 %shard_map.95 = (bf16[4,64,768]{2,1,0:T(8,128)(2,1)S(1)}, f32[4,64,768]{2,1,0:T(8,128)S(1)}, f32[4,8,768]{2,1,0:T(8,128)S(1)}, bf16[4,128,768]{2,1,0:T(8,128)(2,...) custom-call(s32[32]{0:T(128)S(1)} %get-tuple-element.29.codes, ...), custom_call_target="tpu_custom_call" | custom-call | flops 8999999488 | bytes 10000000 | tf_op jit(solution)/shard_map/pallas_call | solution.py:339
  57.1 2.9 %collective-permute-start.6 = (bf16[2,4,192,128]{3,2,1,0:T(8,128)(2,1)S(1)}, bf16[2,4,192,128]{3,2,1,0:T(8,128)(2,1)S(1)}, u32[]{:S(2)}, u32[]{:S(2)}) collective-permute-start(bf16[2,4,192,128]{3,2,1,0:T(8,128)(2,1)S(1)} %get-tuple-element.40), channel_id=1, source_target_pairs={{0,4},{4,0},{1,5},{5,1},{2,6},{6,2},{3,7},{7,3},{8,12},{12,8},{9,1... | collective-permute-start | bytes 1179656 | tf_op jit(solution)/shard_map/ppermute | solution.py:535
  59.9 1.3 %collective-permute-done.6 = bf16[2,4,192,128]{3,2,1,0:T(8,128)(2,1)S(1)} collective-permute-done((bf16[2,4,192,128]{3,2,1,0:T(8,128)(2,1)S(1)}, bf16[2,4,192,128]{3,2,1,0:T(8,128)(2,1)S(1)}, u32[]{:S(2)}, u32[]{:S(2)}) %collective-permute-start.6) | collective-permute-done | bytes 393248 | tf_op jit(solution)/shard_map/ppermute | solution.py:535
  61.3 0.1 add_convert_fusion.edge_sum
  61.4 1.9 %collective-permute-start.7 = (bf16[2,4,192,128]{3,2,1,0:T(8,128)(2,1)S(1)}, bf16[2,4,192,128]{3,2,1,0:T(8,128)(2,1)S(1)}, u32[]{:S(2)}, u32[]{:S(2)}) collective-permute-start(bf16[2,4,192,128]{3,2,1,0:T(8,128)(2,1)S(1)} %add_convert_fusion.edge_sum), channel_id=1, source_target_pairs={{0,32},{32,0},{64,96},{96,64},{128,160},{160,128},{192,224},{224,1... | collective-permute-start | bytes 1179656 | tf_op jit(solution)/shard_map/ppermute | solution.py:537
  63.3 22.8 %shard_map.96 = (bf16[4,4,192,128]{3,2,1,0:T(8,128)(2,1)S(1)}, bf16[4,4,192,128]{3,2,1,0:T(8,128)(2,1)S(1)}, bf16[4,4,192,128]{3,2,1,0:T(8,128)(2,1)S(1)}) custom-call(s32[32]{0:T(128)S(1)} %get-tuple-element.29.codes, bf16[4,4,2,192,128]{4,3,2,1,0:T(8,128)(2,1)} %bitcast.37, bf16[4,4,192,128]{3,2,1,0:T(8,128)(2,1)S(1)} %collective-permute-done.3.mate, ...), custom_call_target="tpu_custom_call" | custom-call | flops 15000000512 | bytes 20000000 | tf_op jit(solution)/shard_map/pallas_call | solution.py:447
  86.1 0.0 collective-permute-done.7.edge_got
  86.1 0.1 collective-permute-start.8
  86.2 2.3 %collective-permute-done.8.got = bf16[4,4,192,128]{3,2,1,0:T(8,128)(2,1)S(1)} collective-permute-done((bf16[4,4,192,128]{3,2,1,0:T(8,128)(2,1)S(1)}, bf16[4,4,192,128]{3,2,1,0:T(8,128)(2,1)S(1)}, u32[]{:S(2)}, u32[]{:S(2)}) %collective-permute-start.8) | collective-permute-done | bytes 786464 | tf_op jit(solution)/shard_map/ppermute | solution.py:540
  88.5 0.8 shard_map.97
  89.3 26.8 %all_to_all.10 = bf16[16,384,128]{2,1,0:T(8,128)(2,1)S(1)} all-to-all(bf16[16,384,128]{2,1,0:T(8,128)(2,1)S(1)} %bitcast.31), channel_id=1, replica_groups=mesh['z'=8,'x'=4,'c'=2,'y'=4] {'x','y'}, dimensions={0} | all-to-all | bytes 3145728 | tf_op jit(solution)/shard_map/all_to_all | solution.py:542
  116.1 2.0 %shard_map.98 = (bf16[192,1024]{1,0:T(8,128)(2,1)}, bf16[192,1024]{1,0:T(8,128)(2,1)}, bf16[192,1024]{1,0:T(8,128)(2,1)}, bf16[192,1024]{1,0:T(8,128)(2,1)}) custom-call(bf16[16,2,192,128]{3,2,1,0:T(8,128)(2,1)S(1)} %bitcast.32), custom_call_target="tpu_custom_call" | custom-call | tf_op jit(solution)/shard_map/pallas_call | solution.py:79
  (3 shorter events, 0.1 us)
Async XLA Ops:
  3.6 7.8 %copy-start.1 = (s32[1,3]{1,0:T(1,128)S(1)}, s32[1,3]{1,0:T(1,128)}, u32[]{:S(2)}) copy-start(s32[1,3]{1,0:T(1,128)} %param.10) | copy-start | bytes 40
  3.6 31.0 %all-to-all-start = ((bf16[16,384,128]{2,1,0:T(8,128)(2,1)}), bf16[16,384,128]{2,1,0:T(8,128)(2,1)S(1)}, u32[]{:S(2)}, u32[]{:S(2)}) async-start(bf16[16,384,128]{2,1,0:T(8,128)(2,1)} %bitcast.38), calls=%async_computation | async-start | bytes 3145728 | tf_op jit(solution)/shard_map/all_to_all | solution.py:525
  11.6 19.9 %collective-permute-start.1 = (s32[5]{0:T(128)S(1)}, s32[5]{0:T(128)S(1)}, u32[]{:S(2)}, u32[]{:S(2)}) collective-permute-start(s32[5]{0:T(128)S(1)} %pad_add_fusion.1), channel_id=1, source_target_pairs={{0,16},{8,24},{16,0},{24,8},{1,17},{9,25},{17,1},{25,9},{2,18},{10... | collective-permute-start | bytes 68 | tf_op jit(solution)/shard_map/ppermute | solution.py:515
  15.1 16.4 %collective-permute-start = (s32[5]{0:T(128)S(1)}, s32[5]{0:T(128)S(1)}, u32[]{:S(2)}, u32[]{:S(2)}) collective-permute-start(s32[5]{0:T(128)S(1)} %pad_add_fusion.1), channel_id=1, source_target_pairs={{0,24},{8,0},{16,8},{24,16},{1,25},{9,1},{17,9},{25,17},{2,26},{10... | collective-permute-start | bytes 68 | tf_op jit(solution)/shard_map/ppermute | solution.py:515
  16.2 15.2 %collective-permute-start.2 = (s32[5]{0:T(128)S(1)}, s32[5]{0:T(128)S(1)}, u32[]{:S(2)}, u32[]{:S(2)}) collective-permute-start(s32[5]{0:T(128)S(1)} %pad_add_fusion.1), channel_id=1, source_target_pairs={{0,8},{8,16},{16,24},{24,0},{1,9},{9,17},{17,25},{25,1},{2,10},{10... | collective-permute-start | bytes 68 | tf_op jit(solution)/shard_map/ppermute | solution.py:515
  34.6 17.2 %copy-start = (bf16[16,384,128]{2,1,0:T(8,128)(2,1)}, bf16[16,384,128]{2,1,0:T(8,128)(2,1)S(1)}, u32[]{:S(2)}) copy-start(bf16[16,384,128]{2,1,0:T(8,128)(2,1)S(1)} %all-to-all-done) | copy-start | bytes 4718596
  34.7 2.4 %collective-permute-start.3 = (bf16[4,4,192,128]{3,2,1,0:T(8,128)(2,1)S(1)}, bf16[4,4,192,128]{3,2,1,0:T(8,128)(2,1)S(1)}, u32[]{:S(2)}, u32[]{:S(2)}) collective-permute-start(bf16[4,4,192,128]{3,2,1,0:T(8,128)(2,1)S(1)} %slice_bitcast_fusion), channel_id=1, source_target_pairs={{0,4},{4,0},{1,5},{5,1},{2,6},{6,2},{3,7},{7,3},{8,12},{12,8},{9,1... | collective-permute-start | bytes 2359304 | tf_op jit(solution)/shard_map/ppermute | solution.py:530
  34.8 17.0 %collective-permute-start.4 = (bf16[2,4,192,128]{3,2,1,0:T(8,128)(2,1)S(1)}, bf16[2,4,192,128]{3,2,1,0:T(8,128)(2,1)S(1)}, u32[]{:S(2)}, u32[]{:S(2)}) collective-permute-start(bf16[2,4,192,128]{3,2,1,0:T(8,128)(2,1)S(1)} %dynamic-slice_bitcast_fusion), channel_id=1, source_target_pairs={{0,32},{32,0},{64,96},{96,64},{128,160},{160,128},{192,224},{224,1... | collective-permute-start | bytes 1179656 | tf_op jit(solution)/shard_map/ppermute | solution.py:529
  51.8 1.8 %collective-permute-start.5 = (bf16[2,4,192,128]{3,2,1,0:T(8,128)(2,1)S(1)}, bf16[2,4,192,128]{3,2,1,0:T(8,128)(2,1)S(1)}, u32[]{:S(2)}, u32[]{:S(2)}) collective-permute-start(bf16[2,4,192,128]{3,2,1,0:T(8,128)(2,1)S(1)} %collective-permute-done.4.edge), channel_id=1, source_target_pairs={{0,4},{4,0},{1,5},{5,1},{2,6},{6,2},{3,7},{7,3},{8,12},{12,8},{9,1... | collective-permute-start | bytes 1179656 | tf_op jit(solution)/shard_map/ppermute | solution.py:533
  57.1 4.2 %collective-permute-start.6 = (bf16[2,4,192,128]{3,2,1,0:T(8,128)(2,1)S(1)}, bf16[2,4,192,128]{3,2,1,0:T(8,128)(2,1)S(1)}, u32[]{:S(2)}, u32[]{:S(2)}) collective-permute-start(bf16[2,4,192,128]{3,2,1,0:T(8,128)(2,1)S(1)} %get-tuple-element.40), channel_id=1, source_target_pairs={{0,4},{4,0},{1,5},{5,1},{2,6},{6,2},{3,7},{7,3},{8,12},{12,8},{9,1... | collective-permute-start | bytes 1179656 | tf_op jit(solution)/shard_map/ppermute | solution.py:535
  61.4 24.7 %collective-permute-start.7 = (bf16[2,4,192,128]{3,2,1,0:T(8,128)(2,1)S(1)}, bf16[2,4,192,128]{3,2,1,0:T(8,128)(2,1)S(1)}, u32[]{:S(2)}, u32[]{:S(2)}) collective-permute-start(bf16[2,4,192,128]{3,2,1,0:T(8,128)(2,1)S(1)} %add_convert_fusion.edge_sum), channel_id=1, source_target_pairs={{0,32},{32,0},{64,96},{96,64},{128,160},{160,128},{192,224},{224,1... | collective-permute-start | bytes 1179656 | tf_op jit(solution)/shard_map/ppermute | solution.py:537
  86.1 2.4 %collective-permute-start.8 = (bf16[4,4,192,128]{3,2,1,0:T(8,128)(2,1)S(1)}, bf16[4,4,192,128]{3,2,1,0:T(8,128)(2,1)S(1)}, u32[]{:S(2)}, u32[]{:S(2)}) collective-permute-start(bf16[4,4,192,128]{3,2,1,0:T(8,128)(2,1)S(1)} %get-tuple-element.43), channel_id=1, source_target_pairs={{0,4},{4,0},{1,5},{5,1},{2,6},{6,2},{3,7},{7,3},{8,12},{12,8},{9,1... | collective-permute-start | bytes 2359304 | tf_op jit(solution)/shard_map/ppermute | solution.py:540

commit v2 on v1

--- a/solution.py
+++ b/solution.py
@@ -58,29 +58,38 @@
 
 
 def pack(*arrays):
+    steps = 2
     return pl.pallas_call(
         pack_kernel,
-        in_specs=[VMEM] * 4,
-        out_specs=VMEM,
+        grid=(steps,),
+        in_specs=[pl.BlockSpec((PIECE // steps, WIDTH), lambda i: (i, 0))] * 4,
+        out_specs=pl.BlockSpec((HEADS, 2, PIECE // steps, PAIR), lambda i: (0, 0, i, 0)),
         out_shape=shape((HEADS, 2, PIECE, PAIR)),
         compiler_params=params(60),
     )(*arrays)
 
 
-def unpack_kernel(in_ref, a_ref, q_ref, k_ref, v_ref):
-    for side, (a, b) in enumerate(((k_ref, v_ref), (a_ref, q_ref))):
+def unpack_kernel(in_ref, a_ref, q_ref, k_ref, v_ref, a, q, k, v, sems):
+    stores = []
+    for side, pairs in enumerate((((k, k_ref), (v, v_ref)), ((a, a_ref), (q, q_ref)))):
         for h in range(HEADS):
             cols = slice(h * HEAD_DIM, (h + 1) * HEAD_DIM)
-            a[:, cols] = in_ref[h, side, :, :HEAD_DIM]
-            b[:, cols] = in_ref[h, side, :, HEAD_DIM:]
+            pairs[0][0][:, cols] = in_ref[h, side, :, :HEAD_DIM]
+            pairs[1][0][:, cols] = in_ref[h, side, :, HEAD_DIM:]
+        for scratch, out in pairs:
+            stores.append(pltpu.make_async_copy(scratch, out, sems.at[len(stores)]))
+            stores[-1].start()
+    for store in stores:
+        store.wait()
 
 
 def unpack(packed):
     return pl.pallas_call(
         unpack_kernel,
         in_specs=[VMEM],
-        out_specs=[VMEM] * 4,
+        out_specs=[HBM] * 4,
         out_shape=[shape((PIECE, WIDTH))] * 4,
+        scratch_shapes=[pltpu.VMEM((PIECE, WIDTH), BF)] * 4 + [pltpu.SemaphoreType.DMA((4,))],
         compiler_params=params(16),
     )(packed)
 
@@ -132,7 +141,7 @@
     p = e.astype(F32) * share
     ds = (p * dprobs).astype(BF)
     dq = dot(kv.T[:HEAD_DIM], ds)
-    return dq, dot(ds, q_side) + dot(p.astype(BF), g_side)
+    return dq, dot(jnp.concatenate([ds, p.astype(BF)], axis=1), jnp.concatenate([q_side, g_side], axis=0))
 
 
 def decode(codes, n):
@@ -167,11 +176,11 @@
     x_ref, rows, arrived, mate, e_out, acc_out, tops_out, codes,
     kv, qg, q_side, scores, top_now, e, acc, tops, sems, e_sems, out_sems,
 ):
-    loads = []
-    for x in range(ROW):
-        loads.append(pltpu.make_async_copy(arrived.at[x, :, 1], qg.at[x], sems.at[x]))
-        loads.append(pltpu.make_async_copy(arrived.at[x, :, 0], kv.at[x], sems.at[ROW + x]))
-    loads.append(pltpu.make_async_copy(mate, kv.at[ROW:NEAR], sems.at[2 * ROW]))
+    loads = [
+        pltpu.make_async_copy(arrived.at[:, :, 1], qg, sems.at[0]),
+        pltpu.make_async_copy(arrived.at[:, :, 0], kv.at[0:ROW], sems.at[1]),
+        pltpu.make_async_copy(mate, kv.at[ROW:NEAR], sems.at[2]),
+    ]
     for load in loads:
         load.start()
     list_pairs(x_ref[0], rows, codes)
@@ -256,9 +265,7 @@
     att_out, dq_out, shares_out, g_t_out, d_edge, d_mate_edge,
     kv, qg, acc, tops, e, scores, top_now, total, dq_sum, q_side, g_side, g_t, att, shares, d_out, sems, out_sems,
 ):
-    loads = []
-    for x in range(ROW):
-        loads.append(pltpu.make_async_copy(arrived.at[x, :, 1], qg.at[x], sems.at[x]))
+    loads = [pltpu.make_async_copy(arrived.at[:, :, 1], qg, sems.at[0])]
     loads.append(pltpu.make_async_copy(edge, kv.at[0:EDGE], sems.at[ROW]))
     loads.append(pltpu.make_async_copy(mate_edge, kv.at[EDGE : 2 * EDGE], sems.at[ROW + 1]))
     loads.append(pltpu.make_async_copy(acc_in, acc, sems.at[ROW + 2]))
@@ -377,11 +384,11 @@
     od_out, d_own, d_mate,
     kv, qg, e, total, dq_sum, q_side, g_side, g_t, att, shares, od, d_out, sems, e_sems, out_sems,
 ):
-    loads = []
-    for x in range(ROW):
-        loads.append(pltpu.make_async_copy(arrived.at[x, :, 1], qg.at[x], sems.at[x]))
-        loads.append(pltpu.make_async_copy(arrived.at[x, :, 0], kv.at[x], sems.at[ROW + x]))
-    loads.append(pltpu.make_async_copy(mate, kv.at[ROW:NEAR], sems.at[2 * ROW]))
+    loads = [
+        pltpu.make_async_copy(arrived.at[:, :, 1], qg, sems.at[0]),
+        pltpu.make_async_copy(arrived.at[:, :, 0], kv.at[0:ROW], sems.at[1]),
+        pltpu.make_async_copy(mate, kv.at[ROW:NEAR], sems.at[2]),
+    ]
     loads.append(pltpu.make_async_copy(g_t_in, g_t, sems.at[2 * ROW + 1]))
     loads.append(pltpu.make_async_copy(shares_in, shares, sems.at[2 * ROW + 2]))
     later = [

time: 119 us -> 116 us (0.975)
  starting transfers between devices: 19.7 us -> 17.7 us
    pallas_call x1, Pallas kernels: 3.47 us -> 6.04 us  [edges(): pl.pallas_call(edge_kernel, in_specs=[SMEM] + [ANY] * 5, out_specs=[ANY]...]
    ppermute x1, starting transfers between devices: 1.92 us -> 0.44 us  [local(): edge_got = lax.ppermute(edge_sum, 'z', rows)]
    pallas_call x1, Pallas kernels: 14.7 us -> 13.4 us  [forward_near(): pl.pallas_call(forward_near_kernel, in_specs=[SMEM] * 2 + [ANY] * 2, out_...]
    pallas_call x1, Pallas kernels: 22.8 us -> 21.6 us  [backward_near(): pl.pallas_call(backward_near_kernel, in_specs=[SMEM, ANY, ANY, HBM] + [AN...]
  transfers between devices with their start and end apart: 10 -> 10, of which waited for: 6 -> 6; matrix products, arithmetic and copies ran while one was open for 0% -> 0% of each run, Pallas kernels for 32% -> 30%
where the time goes in v2:
time: 116 us
  Pallas kernels  46.4 us (40%)
  blocking collectives  26.7 us (23%)
  waiting for transfers between devices  23 us (20%)
  starting transfers between devices  17.7 us (15%)
  between operations  1.59 us (1%)
    all_to_all x1, blocking collectives, local(): lax.all_to_all(out.reshape(HEADS, 2 * PIECE, PAIR), ('x', 'y'), 0, 0, til...  26.7 us
    pallas_call x1, Pallas kernels, backward_near(): pl.pallas_call(backward_near_kernel, in_specs=[SMEM, ANY, ANY, HBM] + [AN...  21.6 us
    ppermute x3, waiting for transfers between devices, block_rows(): lax.ppermute(mine, 'x', [(i, (i - by) % ROW) for i in range(ROW)])  14.3 us
    pallas_call x1, Pallas kernels, forward_near(): pl.pallas_call(forward_near_kernel, in_specs=[SMEM] * 2 + [ANY] * 2, out_...  13.4 us
    all_to_all x1, starting transfers between devices, local(): lax.all_to_all(packed.reshape(HEADS, 2 * PIECE, PAIR), ('x', 'y'), 0, 0,...  7.17 us
    pallas_call x1, Pallas kernels, edges(): pl.pallas_call(edge_kernel, in_specs=[SMEM] + [ANY] * 5, out_specs=[ANY]...  6.04 us
    ppermute x3, starting transfers between devices, block_rows(): lax.ppermute(mine, 'x', [(i, (i - by) % ROW) for i in range(ROW)])  5.48 us
    all_to_all x1, waiting for transfers between devices, local(): lax.all_to_all(packed.reshape(HEADS, 2 * PIECE, PAIR), ('x', 'y'), 0, 0,...  3.11 us
  transfers between devices with their start and end apart: 10, of which 6 were waited for; matrix products, arithmetic and copies ran while one was open for 0% of the time, Pallas kernels for 30%

profile of v2, /device:TPU:64, one launch (start us, length us, event | category | flops | bytes accessed | tf_op | source)
XLA Modules:
  0.0 115.8 jit_solution(16688328257642034879)
XLA Ops:
  0.6 2.7 %shard_map.93 = bf16[16,2,192,128]{3,2,1,0:T(8,128)(2,1)} custom-call(bf16[192,1024]{1,0:T(8,128)(2,1)} %bitcast.39, bf16[192,1024]{1,0:T(8,128)(2,1)} %bitcast.40, bf16[192,1024]{1,0:T(8,128)(2,1)} %bitcast.41, bf16[192,1024]{1,0:T(8,128)(2,1)} %bitcast.42), custom_call_target="tpu_custom_call" | custom-call | tf_op jit(solution)/shard_map/pallas_call | solution.py:62
  3.4 0.0 copy-start.1
  3.4 7.2 %all-to-all-start = ((bf16[16,384,128]{2,1,0:T(8,128)(2,1)}), bf16[16,384,128]{2,1,0:T(8,128)(2,1)S(1)}, u32[]{:S(2)}, u32[]{:S(2)}) async-start(bf16[16,384,128]{2,1,0:T(8,128)(2,1)} %bitcast.38), calls=%async_computation | async-start | bytes 3145728 | tf_op jit(solution)/shard_map/all_to_all | solution.py:532
  11.2 0.0 copy-done.1
  11.2 0.1 pad_add_fusion.1
  11.3 3.5 %collective-permute-start.1 = (s32[5]{0:T(128)S(1)}, s32[5]{0:T(128)S(1)}, u32[]{:S(2)}, u32[]{:S(2)}) collective-permute-start(s32[5]{0:T(128)S(1)} %pad_add_fusion.1), channel_id=1, source_target_pairs={{0,16},{8,24},{16,0},{24,8},{1,17},{9,25},{17,1},{25,9},{2,18},{10... | collective-permute-start | bytes 68 | tf_op jit(solution)/shard_map/ppermute | solution.py:522
  14.8 1.2 %collective-permute-start = (s32[5]{0:T(128)S(1)}, s32[5]{0:T(128)S(1)}, u32[]{:S(2)}, u32[]{:S(2)}) collective-permute-start(s32[5]{0:T(128)S(1)} %pad_add_fusion.1), channel_id=1, source_target_pairs={{0,24},{8,0},{16,8},{24,16},{1,25},{9,1},{17,9},{25,17},{2,26},{10... | collective-permute-start | bytes 68 | tf_op jit(solution)/shard_map/ppermute | solution.py:522
  15.9 0.9 collective-permute-start.2
  16.8 0.1 fusion.5
  16.9 14.3 %collective-permute-done.1 = s32[5]{0:T(128)S(1)} collective-permute-done((s32[5]{0:T(128)S(1)}, s32[5]{0:T(128)S(1)}, u32[]{:S(2)}, u32[]{:S(2)}) %collective-permute-start.1) | collective-permute-done | bytes 52 | tf_op jit(solution)/shard_map/ppermute | solution.py:522
  31.2 0.0 collective-permute-done
  31.2 0.0 collective-permute-done.2
  31.2 3.1 %all-to-all-done = bf16[16,384,128]{2,1,0:T(8,128)(2,1)S(1)} async-done(((bf16[16,384,128]{2,1,0:T(8,128)(2,1)}), bf16[16,384,128]{2,1,0:T(8,128)(2,1)S(1)}, u32[]{:S(2)}, u32[]{:S(2)}) %all-to-all-start) | async-done | bytes 1572896 | tf_op jit(solution)/shard_map/all_to_all | solution.py:532
  34.3 0.0 copy-start
  34.3 0.1 slice_bitcast_fusion
  34.4 0.1 collective-permute-start.3
  34.5 2.0 %collective-permute-start.4 = (bf16[2,4,192,128]{3,2,1,0:T(8,128)(2,1)S(1)}, bf16[2,4,192,128]{3,2,1,0:T(8,128)(2,1)S(1)}, u32[]{:S(2)}, u32[]{:S(2)}) collective-permute-start(bf16[2,4,192,128]{3,2,1,0:T(8,128)(2,1)S(1)} %dynamic-slice_bitcast_fusion), channel_id=1, source_target_pairs={{0,32},{32,0},{64,96},{96,64},{128,160},{160,128},{192,224},{224,1... | collective-permute-start | bytes 1179656 | tf_op jit(solution)/shard_map/ppermute | solution.py:536
  36.5 0.2 collective-permute-done.3.mate
  36.7 13.4 %shard_map.94 = (bf16[4,4,768,768]{3,2,1,0:T(8,128)(2,1)}, f32[4,80,768]{2,1,0:T(8,128)S(1)}, f32[4,8,768]{2,1,0:T(8,128)S(1)}, s32[32]{0:T(128)S(1)}) custom-call(s32[1]{0:T(128)} %bitcast.1.x_ref, s32[4,5]{1,0:T(4,128)S(1)} %pad_add_fusion.rows, bf16[4,4,2,192,128]{4,3,2,1,0:T(8,128)(2,1)S(1)} %bitcast.35, ...), custom_call_target="tpu_custom_call" | custom-call | flops 8999999488 | bytes 20000000 | tf_op jit(solution)/shard_map/pallas_call | solution.py:235
  50.2 0.0 copy-done
  50.2 0.0 collective-permute-done.4.edge
  50.2 0.1 collective-permute-start.5
  50.3 1.7 %collective-permute-done.5.mate_edge = bf16[2,4,192,128]{3,2,1,0:T(8,128)(2,1)S(1)} collective-permute-done((bf16[2,4,192,128]{3,2,1,0:T(8,128)(2,1)S(1)}, bf16[2,4,192,128]{3,2,1,0:T(8,128)(2,1)S(1)}, u32[]{:S(2)}, u32[]{:S(2)}) %collective-permute-start.5) | collective-permute-done | bytes 393248 | tf_op jit(solution)/shard_map/ppermute | solution.py:540
  52.0 6.0 %shard_map.95 = (bf16[4,64,768]{2,1,0:T(8,128)(2,1)S(1)}, f32[4,64,768]{2,1,0:T(8,128)S(1)}, f32[4,8,768]{2,1,0:T(8,128)S(1)}, bf16[4,128,768]{2,1,0:T(8,128)(2,...) custom-call(s32[32]{0:T(128)S(1)} %get-tuple-element.29.codes, ...), custom_call_target="tpu_custom_call" | custom-call | flops 8999999488 | bytes 10000000 | tf_op jit(solution)/shard_map/pallas_call | solution.py:346
  58.1 2.4 %collective-permute-start.6 = (bf16[2,4,192,128]{3,2,1,0:T(8,128)(2,1)S(1)}, bf16[2,4,192,128]{3,2,1,0:T(8,128)(2,1)S(1)}, u32[]{:S(2)}, u32[]{:S(2)}) collective-permute-start(bf16[2,4,192,128]{3,2,1,0:T(8,128)(2,1)S(1)} %get-tuple-element.40), channel_id=1, source_target_pairs={{0,4},{4,0},{1,5},{5,1},{2,6},{6,2},{3,7},{7,3},{8,12},{12,8},{9,1... | collective-permute-start | bytes 1179656 | tf_op jit(solution)/shard_map/ppermute | solution.py:542
  60.4 1.3 %collective-permute-done.6 = bf16[2,4,192,128]{3,2,1,0:T(8,128)(2,1)S(1)} collective-permute-done((bf16[2,4,192,128]{3,2,1,0:T(8,128)(2,1)S(1)}, bf16[2,4,192,128]{3,2,1,0:T(8,128)(2,1)S(1)}, u32[]{:S(2)}, u32[]{:S(2)}) %collective-permute-start.6) | collective-permute-done | bytes 393248 | tf_op jit(solution)/shard_map/ppermute | solution.py:542
  61.8 0.1 add_convert_fusion.edge_sum
  61.9 0.4 collective-permute-start.7
  62.3 21.6 %shard_map.96 = (bf16[4,4,192,128]{3,2,1,0:T(8,128)(2,1)S(1)}, bf16[4,4,192,128]{3,2,1,0:T(8,128)(2,1)S(1)}, bf16[4,4,192,128]{3,2,1,0:T(8,128)(2,1)S(1)}) custom-call(s32[32]{0:T(128)S(1)} %get-tuple-element.29.codes, bf16[4,4,2,192,128]{4,3,2,1,0:T(8,128)(2,1)} %bitcast.37, bf16[4,4,192,128]{3,2,1,0:T(8,128)(2,1)S(1)} %collective-permute-done.3.mate, ...), custom_call_target="tpu_custom_call" | custom-call | flops 15000000512 | bytes 20000000 | tf_op jit(solution)/shard_map/pallas_call | solution.py:454
  83.9 0.0 collective-permute-done.7.edge_got
  84.0 0.1 collective-permute-start.8
  84.1 2.3 %collective-permute-done.8.got = bf16[4,4,192,128]{3,2,1,0:T(8,128)(2,1)S(1)} collective-permute-done((bf16[4,4,192,128]{3,2,1,0:T(8,128)(2,1)S(1)}, bf16[4,4,192,128]{3,2,1,0:T(8,128)(2,1)S(1)}, u32[]{:S(2)}, u32[]{:S(2)}) %collective-permute-start.8) | collective-permute-done | bytes 786464 | tf_op jit(solution)/shard_map/ppermute | solution.py:547
  86.3 0.8 shard_map.97
  87.1 26.7 %all_to_all.10 = bf16[16,384,128]{2,1,0:T(8,128)(2,1)S(1)} all-to-all(bf16[16,384,128]{2,1,0:T(8,128)(2,1)S(1)} %bitcast.31), channel_id=1, replica_groups=mesh['z'=8,'x'=4,'c'=2,'y'=4] {'x','y'}, dimensions={0} | all-to-all | bytes 3145728 | tf_op jit(solution)/shard_map/all_to_all | solution.py:549
  113.8 1.8 %shard_map.98 = (bf16[192,1024]{1,0:T(8,128)(2,1)}, bf16[192,1024]{1,0:T(8,128)(2,1)}, bf16[192,1024]{1,0:T(8,128)(2,1)}, bf16[192,1024]{1,0:T(8,128)(2,1)}) custom-call(bf16[16,2,192,128]{3,2,1,0:T(8,128)(2,1)S(1)} %bitcast.32), custom_call_target="tpu_custom_call" | custom-call | tf_op jit(solution)/shard_map/pallas_call | solution.py:87
  (3 shorter events, 0.1 us)
Async XLA Ops:
  3.4 7.8 %copy-start.1 = (s32[1,3]{1,0:T(1,128)S(1)}, s32[1,3]{1,0:T(1,128)}, u32[]{:S(2)}) copy-start(s32[1,3]{1,0:T(1,128)} %param.10) | copy-start | bytes 40
  3.4 31.0 %all-to-all-start = ((bf16[16,384,128]{2,1,0:T(8,128)(2,1)}), bf16[16,384,128]{2,1,0:T(8,128)(2,1)S(1)}, u32[]{:S(2)}, u32[]{:S(2)}) async-start(bf16[16,384,128]{2,1,0:T(8,128)(2,1)} %bitcast.38), calls=%async_computation | async-start | bytes 3145728 | tf_op jit(solution)/shard_map/all_to_all | solution.py:532
  11.3 19.9 %collective-permute-start.1 = (s32[5]{0:T(128)S(1)}, s32[5]{0:T(128)S(1)}, u32[]{:S(2)}, u32[]{:S(2)}) collective-permute-start(s32[5]{0:T(128)S(1)} %pad_add_fusion.1), channel_id=1, source_target_pairs={{0,16},{8,24},{16,0},{24,8},{1,17},{9,25},{17,1},{25,9},{2,18},{10... | collective-permute-start | bytes 68 | tf_op jit(solution)/shard_map/ppermute | solution.py:522
  14.8 16.4 %collective-permute-start = (s32[5]{0:T(128)S(1)}, s32[5]{0:T(128)S(1)}, u32[]{:S(2)}, u32[]{:S(2)}) collective-permute-start(s32[5]{0:T(128)S(1)} %pad_add_fusion.1), channel_id=1, source_target_pairs={{0,24},{8,0},{16,8},{24,16},{1,25},{9,1},{17,9},{25,17},{2,26},{10... | collective-permute-start | bytes 68 | tf_op jit(solution)/shard_map/ppermute | solution.py:522
  15.9 15.2 %collective-permute-start.2 = (s32[5]{0:T(128)S(1)}, s32[5]{0:T(128)S(1)}, u32[]{:S(2)}, u32[]{:S(2)}) collective-permute-start(s32[5]{0:T(128)S(1)} %pad_add_fusion.1), channel_id=1, source_target_pairs={{0,8},{8,16},{16,24},{24,0},{1,9},{9,17},{17,25},{25,1},{2,10},{10... | collective-permute-start | bytes 68 | tf_op jit(solution)/shard_map/ppermute | solution.py:522
  34.3 15.9 %copy-start = (bf16[16,384,128]{2,1,0:T(8,128)(2,1)}, bf16[16,384,128]{2,1,0:T(8,128)(2,1)S(1)}, u32[]{:S(2)}) copy-start(bf16[16,384,128]{2,1,0:T(8,128)(2,1)S(1)} %all-to-all-done) | copy-start | bytes 4718596
  34.4 2.4 %collective-permute-start.3 = (bf16[4,4,192,128]{3,2,1,0:T(8,128)(2,1)S(1)}, bf16[4,4,192,128]{3,2,1,0:T(8,128)(2,1)S(1)}, u32[]{:S(2)}, u32[]{:S(2)}) collective-permute-start(bf16[4,4,192,128]{3,2,1,0:T(8,128)(2,1)S(1)} %slice_bitcast_fusion), channel_id=1, source_target_pairs={{0,4},{4,0},{1,5},{5,1},{2,6},{6,2},{3,7},{7,3},{8,12},{12,8},{9,1... | collective-permute-start | bytes 2359304 | tf_op jit(solution)/shard_map/ppermute | solution.py:537
  34.5 15.7 %collective-permute-start.4 = (bf16[2,4,192,128]{3,2,1,0:T(8,128)(2,1)S(1)}, bf16[2,4,192,128]{3,2,1,0:T(8,128)(2,1)S(1)}, u32[]{:S(2)}, u32[]{:S(2)}) collective-permute-start(bf16[2,4,192,128]{3,2,1,0:T(8,128)(2,1)S(1)} %dynamic-slice_bitcast_fusion), channel_id=1, source_target_pairs={{0,32},{32,0},{64,96},{96,64},{128,160},{160,128},{192,224},{224,1... | collective-permute-start | bytes 1179656 | tf_op jit(solution)/shard_map/ppermute | solution.py:536
  50.2 1.8 %collective-permute-start.5 = (bf16[2,4,192,128]{3,2,1,0:T(8,128)(2,1)S(1)}, bf16[2,4,192,128]{3,2,1,0:T(8,128)(2,1)S(1)}, u32[]{:S(2)}, u32[]{:S(2)}) collective-permute-start(bf16[2,4,192,128]{3,2,1,0:T(8,128)(2,1)S(1)} %collective-permute-done.4.edge), channel_id=1, source_target_pairs={{0,4},{4,0},{1,5},{5,1},{2,6},{6,2},{3,7},{7,3},{8,12},{12,8},{9,1... | collective-permute-start | bytes 1179656 | tf_op jit(solution)/shard_map/ppermute | solution.py:540
  58.1 3.7 %collective-permute-start.6 = (bf16[2,4,192,128]{3,2,1,0:T(8,128)(2,1)S(1)}, bf16[2,4,192,128]{3,2,1,0:T(8,128)(2,1)S(1)}, u32[]{:S(2)}, u32[]{:S(2)}) collective-permute-start(bf16[2,4,192,128]{3,2,1,0:T(8,128)(2,1)S(1)} %get-tuple-element.40), channel_id=1, source_target_pairs={{0,4},{4,0},{1,5},{5,1},{2,6},{6,2},{3,7},{7,3},{8,12},{12,8},{9,1... | collective-permute-start | bytes 1179656 | tf_op jit(solution)/shard_map/ppermute | solution.py:542
  61.9 22.0 %collective-permute-start.7 = (bf16[2,4,192,128]{3,2,1,0:T(8,128)(2,1)S(1)}, bf16[2,4,192,128]{3,2,1,0:T(8,128)(2,1)S(1)}, u32[]{:S(2)}, u32[]{:S(2)}) collective-permute-start(bf16[2,4,192,128]{3,2,1,0:T(8,128)(2,1)S(1)} %add_convert_fusion.edge_sum), channel_id=1, source_target_pairs={{0,32},{32,0},{64,96},{96,64},{128,160},{160,128},{192,224},{224,1... | collective-permute-start | bytes 1179656 | tf_op jit(solution)/shard_map/ppermute | solution.py:544
  84.0 2.4 %collective-permute-start.8 = (bf16[4,4,192,128]{3,2,1,0:T(8,128)(2,1)S(1)}, bf16[4,4,192,128]{3,2,1,0:T(8,128)(2,1)S(1)}, u32[]{:S(2)}, u32[]{:S(2)}) collective-permute-start(bf16[4,4,192,128]{3,2,1,0:T(8,128)(2,1)S(1)} %get-tuple-element.43), channel_id=1, source_target_pairs={{0,4},{4,0},{1,5},{5,1},{2,6},{6,2},{3,7},{7,3},{8,12},{12,8},{9,1... | collective-permute-start | bytes 2359304 | tf_op jit(solution)/shard_map/ppermute | solution.py:547

commit v3 on v2

--- a/solution.py
+++ b/solution.py
@@ -202,7 +202,7 @@
     count = codes[NEAR_COUNT]
     score(0, 0)
 
-    def one_pair(n, carry):
+    def one_pair(n, following):
         ring = n % 2
         j, b, i = decode(codes, n)
 
@@ -212,13 +212,18 @@
 
         top = top_now[ring]
         e[ring], part = values_of(flat(kv.at[i]), scores[ring], top)
-        score(jnp.minimum(n + 1, count - 1), 1 - ring)
+        if following:
+            score(n + 1, 1 - ring)
         merge(acc, j, part, top)
         tops[j, pl.ds(b, 1), :] = top
         store(j, b, ring).start()
+
+    def step(n, carry):
+        one_pair(n, True)
         return carry
 
-    lax.fori_loop(0, count, one_pair, 0)
+    lax.fori_loop(0, count - 1, step, 0)
+    one_pair(count - 1, False)
     outs = [
         pltpu.make_async_copy(acc, acc_out, out_sems.at[0]),
         pltpu.make_async_copy(tops, tops_out, out_sems.at[1]),
@@ -380,7 +385,7 @@
 
 
 def backward_near_kernel(
-    codes, arrived, mate, e_in, att_in, dq_in, shares_in, g_t_in, edge_sum,
+    codes, arrived, mate, e_in, att_in, dq_in, shares_in, g_t_in,
     od_out, d_own, d_mate,
     kv, qg, e, total, dq_sum, q_side, g_side, g_t, att, shares, od, d_out, sems, e_sems, out_sems,
 ):
@@ -450,10 +455,10 @@
         store.wait()
 
 
-def backward_near(codes, arrived, mate, e, att, dq, shares, g_t, edge_sum):
+def backward_near(codes, arrived, mate, e, att, dq, shares, g_t):
     return pl.pallas_call(
         backward_near_kernel,
-        in_specs=[SMEM, ANY, ANY, HBM] + [ANY] * 5,
+        in_specs=[SMEM, ANY, ANY, HBM] + [ANY] * 4,
         out_specs=[ANY] * 3,
         out_shape=[shape(block(ROW))] * 3,
         scratch_shapes=[
@@ -475,17 +480,17 @@
         ],
         compiler_params=params(KERNEL_MIB),
         cost_estimate=cost(15 * 10**9, 20 * 10**6),
-    )(codes, arrived, mate, e, att, dq, shares, g_t, edge_sum)
-
-
-def fold_kernel(upper, own, got, edge_got, od, out, sums, sems, od_sem):
+    )(codes, arrived, mate, e, att, dq, shares, g_t)
+
+
+def fold_kernel(upper, own, got, edge_got, mate_edge_got, od, out, sums, sems, od_sem):
     kept = pltpu.make_async_copy(od, out.at[:, :, 1], od_sem)
     kept.start()
     stores = []
     for x in range(ROW):
         total = own[x].astype(F32) + got[x].astype(F32)
         listed = upper[0] == (0 if x >= EDGE else 1)
-        far = edge_got[x % EDGE].astype(F32)
+        far = edge_got[x % EDGE].astype(F32) + mate_edge_got[x % EDGE].astype(F32)
         sums[x] = (total + jnp.where(listed, far, jnp.zeros_like(far))).astype(BF)
         stores.append(pltpu.make_async_copy(sums.at[x], out.at[x, :, 0], sems.at[x]))
         stores[x].start()
@@ -494,10 +499,10 @@
     kept.wait()
 
 
-def fold(upper, own, got, edge_got, od):
+def fold(upper, own, got, edge_got, mate_edge_got, od):
     return pl.pallas_call(
         fold_kernel,
-        in_specs=[SMEM, VMEM, VMEM, VMEM, ANY],
+        in_specs=[SMEM, VMEM, VMEM, VMEM, VMEM, ANY],
         out_specs=HBM,
         out_shape=shape((ROW, QUARTERS, 2, PIECE, PAIR)),
         scratch_shapes=[
@@ -506,7 +511,7 @@
             pltpu.SemaphoreType.DMA,
         ],
         compiler_params=params(16),
-    )(upper, own, got, edge_got, od)
+    )(upper, own, got, edge_got, mate_edge_got, od)
 
 
 def block_rows(nbr_views, nbr_counts):
@@ -539,13 +544,13 @@
     edge, acc = lax.optimization_barrier((edge, acc))
     mate_edge = lax.ppermute(edge, "c", cores)
     att, dq, shares, g_t, d_edge, d_mate_edge = edges(codes, arrived, edge, mate_edge, acc, tops)
-    edge_sum = d_edge.astype(F32) + lax.ppermute(d_mate_edge, "c", cores).astype(F32)
-    edge_sum = edge_sum.astype(BF)
-    edge_got = lax.ppermute(edge_sum, "z", rows)
-    od, d_own, d_mate = backward_near(codes, arrived, mate, e, att, dq, shares, g_t, edge_sum)
-    d_mate, edge_got = lax.optimization_barrier((d_mate, edge_got))
+    edge_got = lax.ppermute(d_edge, "z", rows)
+    across = [(2 * i + c, 2 * (i ^ 1) + 1 - c) for i in range(lax.axis_size("z")) for c in range(2)]
+    mate_edge_got = lax.ppermute(d_mate_edge, ("z", "c"), across)
+    od, d_own, d_mate = backward_near(codes, arrived, mate, e, att, dq, shares, g_t)
+    d_mate, edge_got, mate_edge_got = lax.optimization_barrier((d_mate, edge_got, mate_edge_got))
     got = lax.ppermute(d_mate, "c", cores)
-    out = fold(upper.astype(jnp.int32)[None], d_own, got, edge_got, od)
+    out = fold(upper.astype(jnp.int32)[None], d_own, got, edge_got, mate_edge_got, od)
     back = lax.all_to_all(out.reshape(HEADS, 2 * PIECE, PAIR), ("x", "y"), 0, 0, tiled=True)
     results = unpack(back.reshape(HEADS, 2, PIECE, PAIR))
     return tuple(result[None] for result in results)

time: 116 us -> 117 us (level)
  the two profiles are of different devices: /device:TPU:64 before, /device:TPU:192 now
where the time goes in v3:
time: 117 us; the launch traced here: 115 us
  Pallas kernels  43.9 us (38%)
  blocking collectives  26.8 us (23%)
  waiting for transfers between devices  22.5 us (19%)
  starting transfers between devices  20.4 us (17%)
  between operations  1.59 us (1%)
    all_to_all x1, blocking collectives, local(): lax.all_to_all(out.reshape(HEADS, 2 * PIECE, PAIR), ('x', 'y'), 0, 0, til...  26.8 us
    pallas_call x1, Pallas kernels, backward_near(): pl.pallas_call(backward_near_kernel, in_specs=[SMEM, ANY, ANY, HBM] + [AN...  21.6 us
    ppermute x3, waiting for transfers between devices, block_rows(): lax.ppermute(mine, 'x', [(i, (i - by) % ROW) for i in range(ROW)])  14.3 us
    pallas_call x1, Pallas kernels, forward_near(): pl.pallas_call(forward_near_kernel, in_specs=[SMEM] * 2 + [ANY] * 2, out_...  13.4 us
    all_to_all x1, starting transfers between devices, local(): lax.all_to_all(packed.reshape(HEADS, 2 * PIECE, PAIR), ('x', 'y'), 0, 0,...  7.17 us
    ppermute x3, starting transfers between devices, block_rows(): lax.ppermute(mine, 'x', [(i, (i - by) % ROW) for i in range(ROW)])  5.48 us
    ppermute x1, starting transfers between devices, local(): mate_edge_got = lax.ppermute(d_mate_edge, ('z', 'c'), across)  4.2 us
    pallas_call x1, Pallas kernels, edges(): pl.pallas_call(edge_kernel, in_specs=[SMEM] + [ANY] * 5, out_specs=[ANY]...  3.38 us
  transfers between devices with their start and end apart: 10, of which 5 were waited for; matrix products, arithmetic and copies ran while one was open for 0% of the time, Pallas kernels for 30%

profile of v3, /device:TPU:192, one launch (start us, length us, event | category | flops | bytes accessed | tf_op | source)
XLA Modules:
  0.0 115.4 jit_solution(605405754013534675)
XLA Ops:
  0.6 2.7 %shard_map.93 = bf16[16,2,192,128]{3,2,1,0:T(8,128)(2,1)} custom-call(bf16[192,1024]{1,0:T(8,128)(2,1)} %bitcast.39, bf16[192,1024]{1,0:T(8,128)(2,1)} %bitcast.40, bf16[192,1024]{1,0:T(8,128)(2,1)} %bitcast.41, bf16[192,1024]{1,0:T(8,128)(2,1)} %bitcast.42), custom_call_target="tpu_custom_call" | custom-call | tf_op jit(solution)/shard_map/pallas_call | solution.py:62
  3.4 0.0 copy-start.1
  3.4 7.2 %all-to-all-start = ((bf16[16,384,128]{2,1,0:T(8,128)(2,1)}), bf16[16,384,128]{2,1,0:T(8,128)(2,1)S(1)}, u32[]{:S(2)}, u32[]{:S(2)}) async-start(bf16[16,384,128]{2,1,0:T(8,128)(2,1)} %bitcast.38), calls=%async_computation | async-start | bytes 3145728 | tf_op jit(solution)/shard_map/all_to_all | solution.py:537
  11.2 0.0 copy-done.1
  11.2 0.1 pad_add_fusion.1
  11.3 3.5 %collective-permute-start.1 = (s32[5]{0:T(128)S(1)}, s32[5]{0:T(128)S(1)}, u32[]{:S(2)}, u32[]{:S(2)}) collective-permute-start(s32[5]{0:T(128)S(1)} %pad_add_fusion.1), channel_id=1, source_target_pairs={{0,16},{8,24},{16,0},{24,8},{1,17},{9,25},{17,1},{25,9},{2,18},{10... | collective-permute-start | bytes 68 | tf_op jit(solution)/shard_map/ppermute | solution.py:527
  14.8 1.2 %collective-permute-start = (s32[5]{0:T(128)S(1)}, s32[5]{0:T(128)S(1)}, u32[]{:S(2)}, u32[]{:S(2)}) collective-permute-start(s32[5]{0:T(128)S(1)} %pad_add_fusion.1), channel_id=1, source_target_pairs={{0,24},{8,0},{16,8},{24,16},{1,25},{9,1},{17,9},{25,17},{2,26},{10... | collective-permute-start | bytes 68 | tf_op jit(solution)/shard_map/ppermute | solution.py:527
  15.9 0.9 collective-permute-start.2
  16.8 0.1 fusion.5
  16.9 14.3 %collective-permute-done.1 = s32[5]{0:T(128)S(1)} collective-permute-done((s32[5]{0:T(128)S(1)}, s32[5]{0:T(128)S(1)}, u32[]{:S(2)}, u32[]{:S(2)}) %collective-permute-start.1) | collective-permute-done | bytes 52 | tf_op jit(solution)/shard_map/ppermute | solution.py:527
  31.2 0.0 collective-permute-done
  31.2 0.0 collective-permute-done.2
  31.2 3.1 %all-to-all-done = bf16[16,384,128]{2,1,0:T(8,128)(2,1)S(1)} async-done(((bf16[16,384,128]{2,1,0:T(8,128)(2,1)}), bf16[16,384,128]{2,1,0:T(8,128)(2,1)S(1)}, u32[]{:S(2)}, u32[]{:S(2)}) %all-to-all-start) | async-done | bytes 1572896 | tf_op jit(solution)/shard_map/all_to_all | solution.py:537
  34.3 0.0 copy-start
  34.3 0.1 slice_bitcast_fusion
  34.4 0.1 collective-permute-start.3
  34.5 1.1 collective-permute-start.4
  35.6 1.1 collective-permute-done.3.mate
  36.7 13.4 %shard_map.94 = (bf16[4,4,768,768]{3,2,1,0:T(8,128)(2,1)}, f32[4,80,768]{2,1,0:T(8,128)S(1)}, f32[4,8,768]{2,1,0:T(8,128)S(1)}, s32[32]{0:T(128)S(1)}) custom-call(s32[1]{0:T(128)} %bitcast.1.x_ref, s32[4,5]{1,0:T(4,128)S(1)} %pad_add_fusion.rows, bf16[4,4,2,192,128]{4,3,2,1,0:T(8,128)(2,1)S(1)} %bitcast.35, ...), custom_call_target="tpu_custom_call" | custom-call | flops 8999999488 | bytes 20000000 | tf_op jit(solution)/shard_map/pallas_call | solution.py:240
  50.2 0.0 copy-done
  50.2 0.0 collective-permute-done.4.edge
  50.2 0.1 collective-permute-start.5
  50.3 1.7 %collective-permute-done.5.mate_edge = bf16[2,4,192,128]{3,2,1,0:T(8,128)(2,1)S(1)} collective-permute-done((bf16[2,4,192,128]{3,2,1,0:T(8,128)(2,1)S(1)}, bf16[2,4,192,128]{3,2,1,0:T(8,128)(2,1)S(1)}, u32[]{:S(2)}, u32[]{:S(2)}) %collective-permute-start.5) | collective-permute-done | bytes 393248 | tf_op jit(solution)/shard_map/ppermute | solution.py:545
  52.0 3.4 %shard_map.95 = (bf16[4,64,768]{2,1,0:T(8,128)(2,1)S(1)}, f32[4,64,768]{2,1,0:T(8,128)S(1)}, f32[4,8,768]{2,1,0:T(8,128)S(1)}, bf16[4,128,768]{2,1,0:T(8,128)(2,...) custom-call(s32[32]{0:T(128)S(1)} %get-tuple-element.30.codes, ...), custom_call_target="tpu_custom_call" | custom-call | flops 8999999488 | bytes 10000000 | tf_op jit(solution)/shard_map/pallas_call | solution.py:351
  55.4 2.2 %collective-permute-start.6 = (bf16[2,4,192,128]{3,2,1,0:T(8,128)(2,1)S(1)}, bf16[2,4,192,128]{3,2,1,0:T(8,128)(2,1)S(1)}, u32[]{:S(2)}, u32[]{:S(2)}) collective-permute-start(bf16[2,4,192,128]{3,2,1,0:T(8,128)(2,1)S(1)} %get-tuple-element.42), channel_id=1, source_target_pairs={{0,32},{32,0},{64,96},{96,64},{128,160},{160,128},{192,224},{224,1... | collective-permute-start | bytes 1179656 | tf_op jit(solution)/shard_map/ppermute | solution.py:547
  57.6 4.2 %collective-permute-start.7 = (bf16[2,4,192,128]{3,2,1,0:T(8,128)(2,1)S(1)}, bf16[2,4,192,128]{3,2,1,0:T(8,128)(2,1)S(1)}, u32[]{:S(2)}, u32[]{:S(2)}) collective-permute-start(bf16[2,4,192,128]{3,2,1,0:T(8,128)(2,1)S(1)} %get-tuple-element.43), channel_id=1, source_target_pairs={{0,36},{4,32},{32,4},{36,0},{64,100},{68,96},{96,68},{100,64},{128... | collective-permute-start | bytes 1179656 | tf_op jit(solution)/shard_map/ppermute | solution.py:549
  61.8 21.6 %shard_map.96 = (bf16[4,4,192,128]{3,2,1,0:T(8,128)(2,1)S(1)}, bf16[4,4,192,128]{3,2,1,0:T(8,128)(2,1)S(1)}, bf16[4,4,192,128]{3,2,1,0:T(8,128)(2,1)S(1)}) custom-call(s32[32]{0:T(128)S(1)} %get-tuple-element.30.codes, bf16[4,4,2,192,128]{4,3,2,1,0:T(8,128)(2,1)} %bitcast.37, bf16[4,4,192,128]{3,2,1,0:T(8,128)(2,1)S(1)} %collective-permute-done.3.mate, ...), custom_call_target="tpu_custom_call" | custom-call | flops 15000000512 | bytes 20000000 | tf_op jit(solution)/shard_map/pallas_call | solution.py:459
  83.4 0.0 collective-permute-done.6.edge_got
  83.4 0.0 collective-permute-done.7.mate_edge_got
  83.4 0.1 collective-permute-start.8
  83.5 2.3 %collective-permute-done.8.got = bf16[4,4,192,128]{3,2,1,0:T(8,128)(2,1)S(1)} collective-permute-done((bf16[4,4,192,128]{3,2,1,0:T(8,128)(2,1)S(1)}, bf16[4,4,192,128]{3,2,1,0:T(8,128)(2,1)S(1)}, u32[]{:S(2)}, u32[]{:S(2)}) %collective-permute-start.8) | collective-permute-done | bytes 786464 | tf_op jit(solution)/shard_map/ppermute | solution.py:552
  85.8 0.9 shard_map.97
  86.6 26.8 %all_to_all.10 = bf16[16,384,128]{2,1,0:T(8,128)(2,1)S(1)} all-to-all(bf16[16,384,128]{2,1,0:T(8,128)(2,1)S(1)} %bitcast.31), channel_id=1, replica_groups=mesh['z'=8,'x'=4,'c'=2,'y'=4] {'x','y'}, dimensions={0} | all-to-all | bytes 3145728 | tf_op jit(solution)/shard_map/all_to_all | solution.py:554
  113.4 1.8 %shard_map.98 = (bf16[192,1024]{1,0:T(8,128)(2,1)}, bf16[192,1024]{1,0:T(8,128)(2,1)}, bf16[192,1024]{1,0:T(8,128)(2,1)}, bf16[192,1024]{1,0:T(8,128)(2,1)}) custom-call(bf16[16,2,192,128]{3,2,1,0:T(8,128)(2,1)S(1)} %bitcast.32), custom_call_target="tpu_custom_call" | custom-call | tf_op jit(solution)/shard_map/pallas_call | solution.py:87
  (3 shorter events, 0.1 us)
Async XLA Ops:
  3.4 7.8 %copy-start.1 = (s32[1,3]{1,0:T(1,128)S(1)}, s32[1,3]{1,0:T(1,128)}, u32[]{:S(2)}) copy-start(s32[1,3]{1,0:T(1,128)} %param.10) | copy-start | bytes 40
  3.4 31.0 %all-to-all-start = ((bf16[16,384,128]{2,1,0:T(8,128)(2,1)}), bf16[16,384,128]{2,1,0:T(8,128)(2,1)S(1)}, u32[]{:S(2)}, u32[]{:S(2)}) async-start(bf16[16,384,128]{2,1,0:T(8,128)(2,1)} %bitcast.38), calls=%async_computation | async-start | bytes 3145728 | tf_op jit(solution)/shard_map/all_to_all | solution.py:537
  11.3 19.9 %collective-permute-start.1 = (s32[5]{0:T(128)S(1)}, s32[5]{0:T(128)S(1)}, u32[]{:S(2)}, u32[]{:S(2)}) collective-permute-start(s32[5]{0:T(128)S(1)} %pad_add_fusion.1), channel_id=1, source_target_pairs={{0,16},{8,24},{16,0},{24,8},{1,17},{9,25},{17,1},{25,9},{2,18},{10... | collective-permute-start | bytes 68 | tf_op jit(solution)/shard_map/ppermute | solution.py:527
  14.8 16.4 %collective-permute-start = (s32[5]{0:T(128)S(1)}, s32[5]{0:T(128)S(1)}, u32[]{:S(2)}, u32[]{:S(2)}) collective-permute-start(s32[5]{0:T(128)S(1)} %pad_add_fusion.1), channel_id=1, source_target_pairs={{0,24},{8,0},{16,8},{24,16},{1,25},{9,1},{17,9},{25,17},{2,26},{10... | collective-permute-start | bytes 68 | tf_op jit(solution)/shard_map/ppermute | solution.py:527
  15.9 15.2 %collective-permute-start.2 = (s32[5]{0:T(128)S(1)}, s32[5]{0:T(128)S(1)}, u32[]{:S(2)}, u32[]{:S(2)}) collective-permute-start(s32[5]{0:T(128)S(1)} %pad_add_fusion.1), channel_id=1, source_target_pairs={{0,8},{8,16},{16,24},{24,0},{1,9},{9,17},{17,25},{25,1},{2,10},{10... | collective-permute-start | bytes 68 | tf_op jit(solution)/shard_map/ppermute | solution.py:527
  34.3 15.9 %copy-start = (bf16[16,384,128]{2,1,0:T(8,128)(2,1)}, bf16[16,384,128]{2,1,0:T(8,128)(2,1)S(1)}, u32[]{:S(2)}) copy-start(bf16[16,384,128]{2,1,0:T(8,128)(2,1)S(1)} %all-to-all-done) | copy-start | bytes 4718596
  34.4 2.4 %collective-permute-start.3 = (bf16[4,4,192,128]{3,2,1,0:T(8,128)(2,1)S(1)}, bf16[4,4,192,128]{3,2,1,0:T(8,128)(2,1)S(1)}, u32[]{:S(2)}, u32[]{:S(2)}) collective-permute-start(bf16[4,4,192,128]{3,2,1,0:T(8,128)(2,1)S(1)} %slice_bitcast_fusion), channel_id=1, source_target_pairs={{0,4},{4,0},{1,5},{5,1},{2,6},{6,2},{3,7},{7,3},{8,12},{12,8},{9,1... | collective-permute-start | bytes 2359304 | tf_op jit(solution)/shard_map/ppermute | solution.py:542
  34.5 15.7 %collective-permute-start.4 = (bf16[2,4,192,128]{3,2,1,0:T(8,128)(2,1)S(1)}, bf16[2,4,192,128]{3,2,1,0:T(8,128)(2,1)S(1)}, u32[]{:S(2)}, u32[]{:S(2)}) collective-permute-start(bf16[2,4,192,128]{3,2,1,0:T(8,128)(2,1)S(1)} %dynamic-slice_bitcast_fusion), channel_id=1, source_target_pairs={{0,32},{32,0},{64,96},{96,64},{128,160},{160,128},{192,224},{224,1... | collective-permute-start | bytes 1179656 | tf_op jit(solution)/shard_map/ppermute | solution.py:541
  50.2 1.8 %collective-permute-start.5 = (bf16[2,4,192,128]{3,2,1,0:T(8,128)(2,1)S(1)}, bf16[2,4,192,128]{3,2,1,0:T(8,128)(2,1)S(1)}, u32[]{:S(2)}, u32[]{:S(2)}) collective-permute-start(bf16[2,4,192,128]{3,2,1,0:T(8,128)(2,1)S(1)} %collective-permute-done.4.edge), channel_id=1, source_target_pairs={{0,4},{4,0},{1,5},{5,1},{2,6},{6,2},{3,7},{7,3},{8,12},{12,8},{9,1... | collective-permute-start | bytes 1179656 | tf_op jit(solution)/shard_map/ppermute | solution.py:545
  55.4 28.0 %collective-permute-start.6 = (bf16[2,4,192,128]{3,2,1,0:T(8,128)(2,1)S(1)}, bf16[2,4,192,128]{3,2,1,0:T(8,128)(2,1)S(1)}, u32[]{:S(2)}, u32[]{:S(2)}) collective-permute-start(bf16[2,4,192,128]{3,2,1,0:T(8,128)(2,1)S(1)} %get-tuple-element.42), channel_id=1, source_target_pairs={{0,32},{32,0},{64,96},{96,64},{128,160},{160,128},{192,224},{224,1... | collective-permute-start | bytes 1179656 | tf_op jit(solution)/shard_map/ppermute | solution.py:547
  57.6 25.8 %collective-permute-start.7 = (bf16[2,4,192,128]{3,2,1,0:T(8,128)(2,1)S(1)}, bf16[2,4,192,128]{3,2,1,0:T(8,128)(2,1)S(1)}, u32[]{:S(2)}, u32[]{:S(2)}) collective-permute-start(bf16[2,4,192,128]{3,2,1,0:T(8,128)(2,1)S(1)} %get-tuple-element.43), channel_id=1, source_target_pairs={{0,36},{4,32},{32,4},{36,0},{64,100},{68,96},{96,68},{100,64},{128... | collective-permute-start | bytes 1179656 | tf_op jit(solution)/shard_map/ppermute | solution.py:549
  83.4 2.4 %collective-permute-start.8 = (bf16[4,4,192,128]{3,2,1,0:T(8,128)(2,1)S(1)}, bf16[4,4,192,128]{3,2,1,0:T(8,128)(2,1)S(1)}, u32[]{:S(2)}, u32[]{:S(2)}) collective-permute-start(bf16[4,4,192,128]{3,2,1,0:T(8,128)(2,1)S(1)} %get-tuple-element.44), channel_id=1, source_target_pairs={{0,4},{4,0},{1,5},{5,1},{2,6},{6,2},{3,7},{7,3},{8,12},{12,8},{9,1... | collective-permute-start | bytes 2359304 | tf_op jit(solution)/shard_map/ppermute | solution.py:552
